TPU v7x, 512 devices: a whole 4x4x16 slice. The times are simulated.
512 devices in a mesh: loop: 256 (over x_lo, y, z, core), query: 2 (over x_hi).
Axes of the slice: x: 4 (x_hi: 2, x_lo: 2; x = x_hi * 2 + x_lo), y: 4, z: 16, core: 2. Of those that a mesh axis runs over, the one named last changes fastest.
Arguments:
- coefficients: bfloat16 [32, 3, 128], P('query'), may hold values from -0.3125 to 0.3125
- mode_basis: bfloat16 [3, 128, 8192, 128], P(None, None, 'loop'), may hold values from -6 to 6
- shifts: int32 [32, 3], replicated, may hold values from 0 to 8191
- owners: int32 [32], replicated, may hold values from 0 to 1, as said below
Outputs:
- reconstruction: float32 [32, 8192, 128], P('query', 'loop')
- sensor: float32 [32, 8192, 128], P('query', 'loop')
Inputs may be any that keep to these rules, and one draw needn't show every extreme that they name: Each of the 2 owners owns exactly 16 queries.
All inputs are finite; a program needn't handle non-finite values.
Results may differ from a plain program's by a relative error of at most 0.0032.
Values may be sent and summed in bfloat16 or wider, within the bound.
A program may use at most 64 MiB of HBM per device.

v0:
```python
import jax
import jax.numpy as jnp
from jax import lax
from jax.sharding import PartitionSpec as P


def shifted(value, axis, steps):
    count = lax.axis_size(axis)
    pairs = [(source, (source + steps) % count) for source in range(count)]
    return lax.ppermute(value, axis, pairs)


def extended_2(value, sides, width):
    for axis, dim in sides:
        peers, length = (lax.axis_size(axis), value.shape[dim])
        up = [(i, (i + 1) % peers) for i in range(peers)]
        down = [(j, i) for i, j in up]
        last = lax.slice_in_dim(value, length - width, length, axis=dim)
        initial = lax.slice_in_dim(value, 0, width, axis=dim)
        before = lax.ppermute(last, axis, up)
        after = lax.ppermute(initial, axis, down)
        value = jnp.concatenate([before, value, after], axis=dim)
    return value


def take_rows(joined, first_row, length):

    def single(block, begin):
        return lax.dynamic_slice_in_dim(block, begin, length, 0)

    return jax.vmap(jax.vmap(single))(joined, first_row)


def shards(coefficients, mode_basis, shifts, owners):
    per_device = coefficients.shape[0]
    all_queries = shifts.shape[0]
    frames = mode_basis.shape[0]
    modes = mode_basis.shape[1]
    gathered = lax.all_gather(coefficients, "query", axis=0, tiled=True)
    index_here = lax.axis_index("query")
    mine = (owners == index_here).astype(jnp.int32)
    ranks = jnp.cumsum(mine) - 1
    slots = jnp.arange(per_device, dtype=jnp.int32)
    picked = (mine[None, :] == 1) & (ranks[None, :] == slots[:, None])
    chosen = jnp.dot(
        picked.astype(jnp.float32),
        gathered.reshape(all_queries, frames * modes).astype(jnp.float32),
        precision=lax.Precision.HIGHEST,
    )
    chosen = chosen.astype(jnp.bfloat16).reshape(per_device, frames, modes)
    my_shifts = jnp.sum(jnp.where(picked[:, :, None], shifts[None, :, :], 0), axis=1)
    frame_fields = jnp.einsum(
        "qfm,fmxc->qfxc", chosen, mode_basis, preferred_element_type=jnp.float32
    ).astype(jnp.bfloat16)
    slab_rows = frame_fields.shape[2]
    cycle_size = lax.axis_size("loop")
    coarse = my_shifts // slab_rows
    within = my_shifts % slab_rows
    previous = shifted(frame_fields, "loop", 1)
    joined = jnp.concatenate([previous, frame_fields], axis=2)
    aligned = take_rows(joined, slab_rows - within, slab_rows)
    moving = aligned
    distance = 1
    for repeat in range(cycle_size.bit_length()):
        if distance < cycle_size:
            arrived = shifted(moving, "loop", distance)
            taken = (coarse // distance % 2 == 1)[:, :, None, None]
            moving = jnp.where(taken, arrived, moving)
            distance = distance * 2
    summed = jnp.sum(moving.astype(jnp.float32), axis=1)
    extended = extended_2(summed, (("loop", 1),), 1)
    center = extended[:, 1:-1, :]
    upper = extended[:, 2:, :]
    lower = extended[:, :-2, :]
    padded = jnp.pad(center, ((0, 0), (0, 0), (1, 1)))
    right_side = padded[:, :, 2:]
    left_side = padded[:, :, :-2]
    numerator = jnp.abs(upper - 2.0 * center + lower) + jnp.abs(
        right_side - 2.0 * center + left_side
    )
    denominator = jnp.maximum(jnp.abs(upper) + 2.0 * jnp.abs(center) + jnp.abs(lower), 1.0)
    return (center, numerator / denominator)


def solution(mesh):
    placed = (P("query", None, None), P(None, None, "loop", None), P(), P())
    return jax.shard_map(
        shards,
        mesh=mesh,
        in_specs=placed,
        out_specs=(P("query", "loop", None), P("query", "loop", None)),
        check_vma=False,
    )
```

profile of v0, /device:TPU:1, one launch (start us, length us, event | category | flops | bytes accessed | tf_op | source)
XLA Modules:
  0.0 221.1 jit_solution(446994328157167965)
XLA Ops:
  1.7 5.6 %all_gather.3 = bf16[32,3,128]{2,0,1:T(8,128)(2,1)S(1)} all-gather(bf16[16,3,128]{2,0,1:T(8,128)(2,1)} %param.4), channel_id=1, replica_groups=mesh['loop'=256,'query'=2] {'query'}, dimensions={0}, use_global_device_ids=true | all-gather | bytes 36864 | tf_op jit(solution)/shard_map/all_gather | solution.py:39
  8.5 5.4 %collective-permute-start = (bf16[16,3,32,128]{3,0,2,1:T(8,128)(2,1)S(1)}, bf16[16,3,32,128]{3,0,2,1:T(8,128)(2,1)}, u32[]{:S(2)}, u32[]{:S(2)}) collective-permute-start(bf16[16,3,32,128]{3,0,2,1:T(8,128)(2,1)S(1)} %fusion.5), channel_id=1, source_target_pairs={{0,2},{2,4},{4,6},{6,8},{8,10},{10,12},{12,14},{14,16},{16,18},{18... | collective-permute-start | bytes 1179656 | tf_op jit(solution)/shard_map/ppermute | solution.py:10
  14.4 4.8 %collective-permute-done = bf16[16,3,32,128]{3,0,2,1:T(8,128)(2,1)} collective-permute-done((bf16[16,3,32,128]{3,0,2,1:T(8,128)(2,1)S(1)}, bf16[16,3,32,128]{3,0,2,1:T(8,128)(2,1)}, u32[]{:S(2)}, u32[]{:S(2)}) %collective-permute-start) | collective-permute-done | bytes 393248 | tf_op jit(solution)/shard_map/ppermute | solution.py:10
  21.9 3.5 %gather_fusion = bf16[48,32,128]{2,0,1:T(8,128)(2,1)S(1)} fusion(bf16[16,3,64,128]{3,1,0,2:T(4,128)(2,1)} %copy.49, s32[48]{0:T(128)S(1)} %reshape.324), kind=kCustom, calls=%fused_computation | custom fusion | bytes 787200 | tf_op jit(solution)/shard_map/vmap(vmap())/gather | solution.py:29
  26.2 4.0 %collective-permute-start.1 = (bf16[16,3,32,128]{3,2,1,0:T(8,128)(2,1)}, bf16[16,3,32,128]{3,2,1,0:T(8,128)(2,1)}, u32[]{:S(2)}, u32[]{:S(2)}) collective-permute-start(bf16[16,3,32,128]{3,2,1,0:T(8,128)(2,1)} %bitcast.4), channel_id=1, source_target_pairs={{0,2},{2,4},{4,6},{6,8},{8,10},{10,12},{12,14},{14,16},{16,18},{18... | collective-permute-start | bytes 1179656 | tf_op jit(solution)/shard_map/ppermute | solution.py:10
  30.9 8.9 %collective-permute-done.1 = bf16[16,3,32,128]{3,2,1,0:T(8,128)(2,1)} collective-permute-done((bf16[16,3,32,128]{3,2,1,0:T(8,128)(2,1)}, bf16[16,3,32,128]{3,2,1,0:T(8,128)(2,1)}, u32[]{:S(2)}, u32[]{:S(2)}) %collective-permute-start.1) | collective-permute-done | bytes 393248 | tf_op jit(solution)/shard_map/ppermute | solution.py:10
  41.1 1.9 collective-permute-start.2
  43.7 13.6 %collective-permute-done.2 = bf16[16,3,32,128]{3,2,1,0:T(8,128)(2,1)} collective-permute-done((bf16[16,3,32,128]{3,2,1,0:T(8,128)(2,1)S(1)}, bf16[16,3,32,128]{3,2,1,0:T(8,128)(2,1)}, u32[]{:S(2)}, u32[]{:S(2)}) %collective-permute-start.2) | collective-permute-done | bytes 393248 | tf_op jit(solution)/shard_map/ppermute | solution.py:10
  57.3 1.9 broadcast_select_fusion.1
  59.1 1.9 collective-permute-start.3
  61.8 12.4 %collective-permute-done.3 = bf16[16,3,32,128]{3,2,1,0:T(8,128)(2,1)} collective-permute-done((bf16[16,3,32,128]{3,2,1,0:T(8,128)(2,1)}, bf16[16,3,32,128]{3,2,1,0:T(8,128)(2,1)}, u32[]{:S(2)}, u32[]{:S(2)}) %collective-permute-start.3) | collective-permute-done | bytes 393248 | tf_op jit(solution)/shard_map/ppermute | solution.py:10
  75.5 8.6 %collective-permute-start.4 = (bf16[16,3,32,128]{3,2,1,0:T(8,128)(2,1)S(1)}, bf16[16,3,32,128]{3,2,1,0:T(8,128)(2,1)}, u32[]{:S(2)}, u32[]{:S(2)}) collective-permute-start(bf16[16,3,32,128]{3,2,1,0:T(8,128)(2,1)S(1)} %broadcast_select_fusion.2), channel_id=1, source_target_pairs={{0,16},{2,18},{4,20},{6,22},{8,24},{10,26},{12,28},{14,30},{16,32}... | collective-permute-start | bytes 1179656 | tf_op jit(solution)/shard_map/ppermute | solution.py:10
  84.8 6.5 %collective-permute-done.4 = bf16[16,3,32,128]{3,2,1,0:T(8,128)(2,1)} collective-permute-done((bf16[16,3,32,128]{3,2,1,0:T(8,128)(2,1)S(1)}, bf16[16,3,32,128]{3,2,1,0:T(8,128)(2,1)}, u32[]{:S(2)}, u32[]{:S(2)}) %collective-permute-start.4) | collective-permute-done | bytes 393248 | tf_op jit(solution)/shard_map/ppermute | solution.py:10
  93.1 5.1 %collective-permute-start.5 = (bf16[16,3,32,128]{3,2,1,0:T(8,128)(2,1)}, bf16[16,3,32,128]{3,2,1,0:T(8,128)(2,1)}, u32[]{:S(2)}, u32[]{:S(2)}) collective-permute-start(bf16[16,3,32,128]{3,2,1,0:T(8,128)(2,1)} %broadcast_select_fusion.3), channel_id=1, source_target_pairs={{0,32},{2,34},{4,36},{6,38},{8,40},{10,42},{12,44},{14,46},{16,48}... | collective-permute-start | bytes 1179656 | tf_op jit(solution)/shard_map/ppermute | solution.py:10
  99.0 39.4 %collective-permute-done.5 = bf16[16,3,32,128]{3,2,1,0:T(8,128)(2,1)} collective-permute-done((bf16[16,3,32,128]{3,2,1,0:T(8,128)(2,1)}, bf16[16,3,32,128]{3,2,1,0:T(8,128)(2,1)}, u32[]{:S(2)}, u32[]{:S(2)}) %collective-permute-start.5) | collective-permute-done | bytes 393248 | tf_op jit(solution)/shard_map/ppermute | solution.py:10
  139.7 20.3 %collective-permute-start.6 = (bf16[16,3,32,128]{3,2,1,0:T(8,128)(2,1)S(1)}, bf16[16,3,32,128]{3,2,1,0:T(8,128)(2,1)}, u32[]{:S(2)}, u32[]{:S(2)}) collective-permute-start(bf16[16,3,32,128]{3,2,1,0:T(8,128)(2,1)S(1)} %broadcast_select_fusion.4), channel_id=1, source_target_pairs={{0,64},{2,66},{4,68},{6,70},{8,72},{10,74},{12,76},{14,78},{16,80}... | collective-permute-start | bytes 1179656 | tf_op jit(solution)/shard_map/ppermute | solution.py:10
  160.1 4.6 %collective-permute-done.6 = bf16[16,3,32,128]{3,2,1,0:T(8,128)(2,1)} collective-permute-done((bf16[16,3,32,128]{3,2,1,0:T(8,128)(2,1)S(1)}, bf16[16,3,32,128]{3,2,1,0:T(8,128)(2,1)}, u32[]{:S(2)}, u32[]{:S(2)}) %collective-permute-start.6) | collective-permute-done | bytes 393248 | tf_op jit(solution)/shard_map/ppermute | solution.py:10
  166.0 5.0 %collective-permute-start.7 = (bf16[16,3,32,128]{3,2,1,0:T(8,128)(2,1)S(1)}, bf16[16,3,32,128]{3,2,1,0:T(8,128)(2,1)}, u32[]{:S(2)}, u32[]{:S(2)}) collective-permute-start(bf16[16,3,32,128]{3,2,1,0:T(8,128)(2,1)S(1)} %broadcast_select_fusion.5), channel_id=1, source_target_pairs={{0,128},{2,130},{4,132},{6,134},{8,136},{10,138},{12,140},{14,142}... | collective-permute-start | bytes 1179656 | tf_op jit(solution)/shard_map/ppermute | solution.py:10
  171.1 6.7 %collective-permute-done.7 = bf16[16,3,32,128]{3,2,1,0:T(8,128)(2,1)} collective-permute-done((bf16[16,3,32,128]{3,2,1,0:T(8,128)(2,1)S(1)}, bf16[16,3,32,128]{3,2,1,0:T(8,128)(2,1)}, u32[]{:S(2)}, u32[]{:S(2)}) %collective-permute-start.7) | collective-permute-done | bytes 393248 | tf_op jit(solution)/shard_map/ppermute | solution.py:10
  177.8 1.9 broadcast_select_fusion.6
  179.6 4.6 %collective-permute-start.8 = (bf16[16,3,32,128]{3,2,1,0:T(8,128)(2,1)}, bf16[16,3,32,128]{3,2,1,0:T(8,128)(2,1)S(1)}, u32[]{:S(2)}, u32[]{:S(2)}) collective-permute-start(bf16[16,3,32,128]{3,2,1,0:T(8,128)(2,1)} %broadcast_select_fusion.6), channel_id=1, source_target_pairs={{0,256},{2,258},{4,260},{6,262},{8,264},{10,266},{12,268},{14,270}... | collective-permute-start | bytes 1179656 | tf_op jit(solution)/shard_map/ppermute | solution.py:10
  184.4 5.3 %collective-permute-done.8 = bf16[16,3,32,128]{3,2,1,0:T(8,128)(2,1)S(1)} collective-permute-done((bf16[16,3,32,128]{3,2,1,0:T(8,128)(2,1)}, bf16[16,3,32,128]{3,2,1,0:T(8,128)(2,1)S(1)}, u32[]{:S(2)}, u32[]{:S(2)}) %collective-permute-start.8) | collective-permute-done | bytes 393248 | tf_op jit(solution)/shard_map/ppermute | solution.py:10
  190.9 1.9 collective-permute-start.10
  192.8 26.5 %collective-permute-start.9 = (f32[16,1,128]{2,1,0:T(1,128)S(1)}, f32[16,1,128]{2,1,0:T(1,128)S(1)}, u32[]{:S(2)}, u32[]{:S(2)}) collective-permute-start(f32[16,1,128]{2,1,0:T(1,128)S(1)} %get-tuple-element.5), channel_id=1, source_target_pairs={{2,0},{4,2},{6,4},{8,6},{10,8},{12,10},{14,12},{16,14},{18,16},{20... | collective-permute-start | bytes 24584 | tf_op jit(solution)/shard_map/ppermute | solution.py:21
  (51 shorter events, 19.9 us)
Async XLA Ops:
  0.6 6.9 %copy-start = (bf16[3,128,32,128]{3,2,1,0:T(8,128)(2,1)S(1)}, bf16[3,128,32,128]{3,2,1,0:T(8,128)(2,1)}, u32[]{:S(2)}) copy-start(bf16[3,128,32,128]{3,2,1,0:T(8,128)(2,1)} %param.5) | copy-start | bytes 9437188
  1.5 6.0 %copy-start.5 = (pred[32]{0:T(512)(128)(4,1)}, pred[32]{0:T(512)(128)(4,1)S(1)}, u32[]{:S(2)}) copy-start(pred[32]{0:T(512)(128)(4,1)S(1)} %get-tuple-element.14) | copy-start | bytes 100
  1.7 5.8 %copy-start.3 = (s32[32]{0:T(128)}, s32[32]{0:T(128)S(1)}, u32[]{:S(2)}) copy-start(s32[32]{0:T(128)S(1)} %add_reduce_fusion) | copy-start | bytes 388
  7.5 6.5 %copy-start.7 = (s32[32,3]{0,1:T(4,128)S(1)}, s32[32,3]{0,1:T(4,128)}, u32[]{:S(2)}) copy-start(s32[32,3]{0,1:T(4,128)} %param.6) | copy-start | bytes 1156
  7.5 6.4 %copy-start.4 = (s32[32]{0:T(128)S(1)}, s32[32]{0:T(128)}, u32[]{:S(2)}) copy-start(s32[32]{0:T(128)} %copy-done.3) | copy-start | bytes 388
  7.5 6.4 %copy-start.6 = (pred[32]{0:T(512)(128)(4,1)S(1)}, pred[32]{0:T(512)(128)(4,1)}, u32[]{:S(2)}) copy-start(pred[32]{0:T(512)(128)(4,1)} %copy-done.5) | copy-start | bytes 100
  8.5 10.6 %collective-permute-start = (bf16[16,3,32,128]{3,0,2,1:T(8,128)(2,1)S(1)}, bf16[16,3,32,128]{3,0,2,1:T(8,128)(2,1)}, u32[]{:S(2)}, u32[]{:S(2)}) collective-permute-start(bf16[16,3,32,128]{3,0,2,1:T(8,128)(2,1)S(1)} %fusion.5), channel_id=1, source_target_pairs={{0,2},{2,4},{4,6},{6,8},{8,10},{10,12},{12,14},{14,16},{16,18},{18... | collective-permute-start | bytes 1179656 | tf_op jit(solution)/shard_map/ppermute | solution.py:10
  26.2 13.6 %collective-permute-start.1 = (bf16[16,3,32,128]{3,2,1,0:T(8,128)(2,1)}, bf16[16,3,32,128]{3,2,1,0:T(8,128)(2,1)}, u32[]{:S(2)}, u32[]{:S(2)}) collective-permute-start(bf16[16,3,32,128]{3,2,1,0:T(8,128)(2,1)} %bitcast.4), channel_id=1, source_target_pairs={{0,2},{2,4},{4,6},{6,8},{8,10},{10,12},{12,14},{14,16},{16,18},{18... | collective-permute-start | bytes 1179656 | tf_op jit(solution)/shard_map/ppermute | solution.py:10
  41.1 16.2 %collective-permute-start.2 = (bf16[16,3,32,128]{3,2,1,0:T(8,128)(2,1)S(1)}, bf16[16,3,32,128]{3,2,1,0:T(8,128)(2,1)}, u32[]{:S(2)}, u32[]{:S(2)}) collective-permute-start(bf16[16,3,32,128]{3,2,1,0:T(8,128)(2,1)S(1)} %broadcast_select_fusion), channel_id=1, source_target_pairs={{0,4},{2,6},{4,8},{6,10},{8,12},{10,14},{12,16},{14,18},{16,20},{1... | collective-permute-start | bytes 1179656 | tf_op jit(solution)/shard_map/ppermute | solution.py:10
  59.1 15.1 %collective-permute-start.3 = (bf16[16,3,32,128]{3,2,1,0:T(8,128)(2,1)}, bf16[16,3,32,128]{3,2,1,0:T(8,128)(2,1)}, u32[]{:S(2)}, u32[]{:S(2)}) collective-permute-start(bf16[16,3,32,128]{3,2,1,0:T(8,128)(2,1)} %broadcast_select_fusion.1), channel_id=1, source_target_pairs={{0,8},{2,10},{4,12},{6,14},{8,16},{10,18},{12,20},{14,22},{16,24},... | collective-permute-start | bytes 1179656 | tf_op jit(solution)/shard_map/ppermute | solution.py:10
  75.5 15.8 %collective-permute-start.4 = (bf16[16,3,32,128]{3,2,1,0:T(8,128)(2,1)S(1)}, bf16[16,3,32,128]{3,2,1,0:T(8,128)(2,1)}, u32[]{:S(2)}, u32[]{:S(2)}) collective-permute-start(bf16[16,3,32,128]{3,2,1,0:T(8,128)(2,1)S(1)} %broadcast_select_fusion.2), channel_id=1, source_target_pairs={{0,16},{2,18},{4,20},{6,22},{8,24},{10,26},{12,28},{14,30},{16,32}... | collective-permute-start | bytes 1179656 | tf_op jit(solution)/shard_map/ppermute | solution.py:10
  93.1 45.3 %collective-permute-start.5 = (bf16[16,3,32,128]{3,2,1,0:T(8,128)(2,1)}, bf16[16,3,32,128]{3,2,1,0:T(8,128)(2,1)}, u32[]{:S(2)}, u32[]{:S(2)}) collective-permute-start(bf16[16,3,32,128]{3,2,1,0:T(8,128)(2,1)} %broadcast_select_fusion.3), channel_id=1, source_target_pairs={{0,32},{2,34},{4,36},{6,38},{8,40},{10,42},{12,44},{14,46},{16,48}... | collective-permute-start | bytes 1179656 | tf_op jit(solution)/shard_map/ppermute | solution.py:10
  139.7 20.4 %copy-start.1 = (bf16[16,3,32,128]{3,2,1,0:T(8,128)(2,1)}, bf16[16,3,32,128]{3,2,1,0:T(8,128)(2,1)S(1)}, u32[]{:S(2)}) copy-start(bf16[16,3,32,128]{3,2,1,0:T(8,128)(2,1)S(1)} %broadcast_select_fusion.4) | copy-start | bytes 1179652
  139.7 25.0 %collective-permute-start.6 = (bf16[16,3,32,128]{3,2,1,0:T(8,128)(2,1)S(1)}, bf16[16,3,32,128]{3,2,1,0:T(8,128)(2,1)}, u32[]{:S(2)}, u32[]{:S(2)}) collective-permute-start(bf16[16,3,32,128]{3,2,1,0:T(8,128)(2,1)S(1)} %broadcast_select_fusion.4), channel_id=1, source_target_pairs={{0,64},{2,66},{4,68},{6,70},{8,72},{10,74},{12,76},{14,78},{16,80}... | collective-permute-start | bytes 1179656 | tf_op jit(solution)/shard_map/ppermute | solution.py:10
  166.0 11.8 %collective-permute-start.7 = (bf16[16,3,32,128]{3,2,1,0:T(8,128)(2,1)S(1)}, bf16[16,3,32,128]{3,2,1,0:T(8,128)(2,1)}, u32[]{:S(2)}, u32[]{:S(2)}) collective-permute-start(bf16[16,3,32,128]{3,2,1,0:T(8,128)(2,1)S(1)} %broadcast_select_fusion.5), channel_id=1, source_target_pairs={{0,128},{2,130},{4,132},{6,134},{8,136},{10,138},{12,140},{14,142}... | collective-permute-start | bytes 1179656 | tf_op jit(solution)/shard_map/ppermute | solution.py:10
  179.6 10.0 %collective-permute-start.8 = (bf16[16,3,32,128]{3,2,1,0:T(8,128)(2,1)}, bf16[16,3,32,128]{3,2,1,0:T(8,128)(2,1)S(1)}, u32[]{:S(2)}, u32[]{:S(2)}) collective-permute-start(bf16[16,3,32,128]{3,2,1,0:T(8,128)(2,1)} %broadcast_select_fusion.6), channel_id=1, source_target_pairs={{0,256},{2,258},{4,260},{6,262},{8,264},{10,266},{12,268},{14,270}... | collective-permute-start | bytes 1179656 | tf_op jit(solution)/shard_map/ppermute | solution.py:10
  190.9 30.2 %copy-start.2 = (f32[16,32,128]{2,1,0:T(8,128)}, f32[16,32,128]{2,1,0:T(8,128)S(1)}, u32[]{:S(2)}) copy-start(f32[16,32,128]{2,1,0:T(8,128)S(1)} %convert_reduce_fusion) | copy-start | bytes 786436
  190.9 28.4 %collective-permute-start.10 = (f32[16,1,128]{2,1,0:T(1,128)S(1)}, f32[16,1,128]{2,1,0:T(1,128)S(1)}, u32[]{:S(2)}, u32[]{:S(2)}) collective-permute-start(f32[16,1,128]{2,1,0:T(1,128)S(1)} %get-tuple-element.6), channel_id=1, source_target_pairs={{0,2},{2,4},{4,6},{6,8},{8,10},{10,12},{12,14},{14,16},{16,18},{18... | collective-permute-start | bytes 24584 | tf_op jit(solution)/shard_map/ppermute | solution.py:20
  192.8 27.3 %collective-permute-start.9 = (f32[16,1,128]{2,1,0:T(1,128)S(1)}, f32[16,1,128]{2,1,0:T(1,128)S(1)}, u32[]{:S(2)}, u32[]{:S(2)}) collective-permute-start(f32[16,1,128]{2,1,0:T(1,128)S(1)} %get-tuple-element.5), channel_id=1, source_target_pairs={{2,0},{4,2},{6,4},{8,6},{10,8},{12,10},{14,12},{16,14},{18,16},{20... | collective-permute-start | bytes 24584 | tf_op jit(solution)/shard_map/ppermute | solution.py:21
where the time goes:
time: 225 us; the launch traced here: 221 us
  waiting for transfers between devices  103 us (46%)
  starting transfers between devices  85.2 us (38%)
  other arithmetic  15.6 us (7%)
  local copies, waits for them, and re-layouts  9.63 us (4%)
  blocking collectives  5.62 us (2%)
    ppermute x9, waiting for transfers between devices, shifted(): return lax.ppermute(value, axis, pairs)  102 us
    ppermute x9, starting transfers between devices, shifted(): return lax.ppermute(value, axis, pairs)  56.9 us
    ppermute x1, starting transfers between devices, extended_2(): after = lax.ppermute(initial, axis, down)  26.5 us
    select_n x7, other arithmetic, shards(): moving = jnp.where(taken, arrived, moving)  10.5 us
    all_gather x1, blocking collectives, shards(): gathered = lax.all_gather(coefficients, 'query', axis=0, tiled=True)  5.62 us
    gather x4, local copies, waits for them, and re-layouts, single(): return lax.dynamic_slice_in_dim(block, begin, length, 0)  4.5 us
  transfers between devices with their start and end apart: 11, of which 10 were waited for; matrix products, arithmetic and copies ran while one was open for 2% of the time, Pallas kernels for 0%

commit v1 on v0

v1 whole, which is shorter than its diff:
```python
import functools

import jax
import jax.numpy as jnp
from jax import lax
from jax.experimental import pallas as pl
from jax.experimental.pallas import tpu as pltpu
from jax.sharding import PartitionSpec as P

MESH = pl.DeviceIdType.MESH
RING = 16
LANES = 128
WIDE = 8


def swapped(tiles):
    lane = lax.broadcasted_iota(jnp.int32, tiles[0].shape, 1)
    for bit in range(4):
        step = 1 << bit
        width = step * WIDE
        low = (lane // width) % 2 == 0
        new = [None] * RING
        for i in range(RING):
            if i & step:
                continue
            a, b = tiles[i], tiles[i | step]
            new[i] = jnp.where(low, a, pltpu.roll(b, width, 1))
            new[i | step] = jnp.where(low, pltpu.roll(a, LANES - width, 1), b)
        tiles = new
    return tiles


def kernel(
    coef, pick_own, pick_other, basis, shift, recon, sensor,
    coef_in, raw, modes, s1, r1, s2, r2, long, s3, r3, s4, r4, field,
    basis_sem, coef_send, coef_recv, send1, recv1, own1, send2, recv2, own2,
    send3, recv3, own3, send4, recv4, own4, halo_send, halo_recv,
):
    me = lax.axis_index("loop")
    group = lax.axis_index("query")
    devices = lax.axis_size("loop")
    core = me % 2
    z = (me // 2) % RING
    sup = me // (2 * RING)
    spot = sup * 2 + core
    before = (me + devices - 1) % devices
    after = (me + 1) % devices

    def at_z(i):
        return sup * (2 * RING) + i * 2 + core

    def at_spot(i):
        return (i // 2) * (2 * RING) + z * 2 + i % 2

    frames = basis.shape[0]
    loads = [pltpu.make_async_copy(basis.at[f], raw.at[f], basis_sem.at[f]) for f in range(frames)]
    for load in loads:
        load.start()

    barrier = pltpu.get_barrier_semaphore()

    def greet(d, carry):
        pl.semaphore_signal(barrier, inc=1, device_id={"loop": at_z((z + d) % RING)}, device_id_type=MESH)
        pl.semaphore_signal(barrier, inc=1, device_id={"loop": at_spot((spot + d) % RING)}, device_id_type=MESH)
        return carry

    pl.semaphore_signal(barrier, inc=1, device_id={"query": 1 - group}, device_id_type=MESH)
    pl.semaphore_signal(barrier, inc=1, device_id={"loop": before}, device_id_type=MESH)
    pl.semaphore_signal(barrier, inc=1, device_id={"loop": after}, device_id_type=MESH)
    lax.fori_loop(1, RING, greet, 0)
    pl.semaphore_wait(barrier, 2 * (RING - 1) + 3)

    exchange = pltpu.make_async_remote_copy(
        src_ref=coef, dst_ref=coef_in, send_sem=coef_send, recv_sem=coef_recv,
        device_id={"query": 1 - group}, device_id_type=MESH,
    )
    exchange.start()

    def spread(source, target, here, to, send_sem, recv_sem, own_sem):
        pltpu.make_async_copy(source.at[here], target.at[here], own_sem).start()

        def one(d, carry):
            i = (here + d) % RING
            pltpu.make_async_remote_copy(
                src_ref=source.at[i], dst_ref=target.at[here], send_sem=send_sem, recv_sem=recv_sem,
                device_id={"loop": to(i)}, device_id_type=MESH,
            ).start()
            return carry

        lax.fori_loop(1, RING, one, 0)

    def landed(source, target, here, recv_sem, own_sem):
        pltpu.make_async_copy(source.at[here], target.at[here], own_sem).wait()
        most = target.at[pl.ds(0, RING - 1)]
        pltpu.make_async_copy(most, most, recv_sem).wait()

    def sent(source, send_sem):
        most = source.at[pl.ds(0, RING - 1)]
        pltpu.make_async_copy(most, most, send_sem).wait()

    for f in range(frames):
        loads[f].wait()
        modes[f] = jnp.swapaxes(raw[f], 0, 1)
    exchange.wait()
    chosen = jnp.dot(pick_own[...], coef[...], preferred_element_type=jnp.float32)
    chosen = chosen + jnp.dot(pick_other[...], coef_in[...], preferred_element_type=jnp.float32)
    chosen = chosen.astype(jnp.bfloat16)

    for f in range(frames):
        weights = chosen[:, f * LANES:(f + 1) * LANES]
        for half in range(2):
            tiles = [
                jnp.dot(weights, modes[f, half * RING + x], preferred_element_type=jnp.float32).astype(jnp.bfloat16)
                for x in range(RING)
            ]
            tiles = swapped(tiles)
            for i in range(RING):
                s1[f, i, half] = tiles[i]
        spread(s1.at[f], r1.at[f], z, at_z, send1.at[f], recv1.at[f], own1.at[f])

    for f in range(frames):
        landed(s1.at[f], r1.at[f], z, recv1.at[f], own1.at[f])
        for half in range(2):
            s2[f, :, half] = jnp.swapaxes(r1[f, :, half], 0, 1)
        spread(s2.at[f], r2.at[f], spot, at_spot, send2.at[f], recv2.at[f], own2.at[f])

    for f in range(frames):
        landed(s2.at[f], r2.at[f], spot, recv2.at[f], own2.at[f])
        for c in range(2):
            for half in range(2):
                for i in range(8):
                    part = r2[f, i * 2 + c, half].astype(jnp.float32)
                    long[f, c * 2 + half, i * 16:(i + 1) * 16] = part
                    long[f, c * 2 + half, 128 + i * 16:128 + (i + 1) * 16] = part

    lane = lax.broadcasted_iota(jnp.int32, (128, LANES), 1)
    for j in range(4):
        total = None
        for f in range(frames):
            cells = shift[f]
            rows = cells // 16
            turn = (cells % 16) * WIDE

            def moved(rows):
                low = rows % 4
                down = (rows // 4 + (j < low).astype(jnp.int32)) % 128
                return long[f, (j + 4 - low) % 4, pl.ds(128 - down, 128), :]

            both = jnp.where(lane >= LANES - turn, moved(rows + 1), moved(rows))
            both = pltpu.roll(both, turn, 1)
            total = both if total is None else total + both
        total = total.astype(jnp.bfloat16)
        for i in range(8):
            s3[i * 2 + j // 2, j % 2] = total[i * 16:(i + 1) * 16]

    spread(s3, r3, spot, at_spot, send3, recv3, own3)
    landed(s3, r3, spot, recv3, own3)
    for half in range(2):
        s4[:, half] = jnp.swapaxes(r3[:, half], 0, 1)
    spread(s4, r4, z, at_z, send4, recv4, own4)
    landed(s4, r4, z, recv4, own4)
    for half in range(2):
        tiles = swapped([r4[i, half] for i in range(RING)])
        for i in range(RING):
            field[1 + half * RING + i] = tiles[i]

    length = 2 * RING
    up = pltpu.make_async_remote_copy(
        src_ref=field.at[length], dst_ref=field.at[0], send_sem=halo_send.at[0], recv_sem=halo_recv.at[0],
        device_id={"loop": after}, device_id_type=MESH,
    )
    down = pltpu.make_async_remote_copy(
        src_ref=field.at[1], dst_ref=field.at[length + 1], send_sem=halo_send.at[1], recv_sem=halo_recv.at[1],
        device_id={"loop": before}, device_id_type=MESH,
    )
    up.start()
    down.start()
    recon[...] = jnp.swapaxes(field[1:length + 1].astype(jnp.float32), 0, 1)

    place = lax.broadcasted_iota(jnp.int32, (RING, LANES), 1)

    def sense(x):
        lower = field[x].astype(jnp.float32)
        center = field[x + 1].astype(jnp.float32)
        upper = field[x + 2].astype(jnp.float32)
        right = jnp.where(place == LANES - 1, 0.0, pltpu.roll(center, LANES - 1, 1))
        left = jnp.where(place == 0, 0.0, pltpu.roll(center, 1, 1))
        numerator = jnp.abs(upper - 2.0 * center + lower) + jnp.abs(right - 2.0 * center + left)
        denominator = jnp.maximum(jnp.abs(upper) + 2.0 * jnp.abs(center) + jnp.abs(lower), 1.0)
        return numerator / denominator

    inner = {x: sense(x) for x in range(1, length - 1)}
    up.wait()
    down.wait()
    inner[0] = sense(0)
    inner[length - 1] = sense(length - 1)
    sensor[...] = jnp.swapaxes(jnp.stack([inner[x] for x in range(length)]), 0, 1)

    for f in range(frames):
        sent(s1.at[f], send1.at[f])
        sent(s2.at[f], send2.at[f])
    sent(s3, send3)
    sent(s4, send4)


def shards(coefficients, mode_basis, shifts, owners):
    per_device = coefficients.shape[0]
    frames, modes, rows, cells = mode_basis.shape
    group = lax.axis_index("query")
    me = lax.axis_index("loop")
    spot = (me // (2 * RING)) * 2 + me % 2
    mine = owners == group
    index = jnp.arange(owners.shape[0], dtype=jnp.int32)
    rank = jnp.sum((mine[None, :] & (index[None, :] < index[:, None])).astype(jnp.int32), axis=1)
    slots = jnp.arange(per_device, dtype=jnp.int32)
    picked = mine[None, :] & (rank[None, :] == slots[:, None])
    shift = jnp.sum(jnp.where((mine & (rank == spot))[:, None], shifts, 0), axis=0)
    picked = picked.astype(jnp.bfloat16)
    first, second = picked[:, :per_device], picked[:, per_device:]
    pick_own = jnp.where(group == 0, first, second)
    pick_other = jnp.where(group == 0, second, first)
    bf16, f32 = jnp.bfloat16, jnp.float32
    block = (RING, 2, RING, LANES)
    vmem = pl.BlockSpec(memory_space=pltpu.VMEM)
    dma = pltpu.SemaphoreType.DMA
    recon, sensor = pl.pallas_call(
        kernel,
        out_shape=[jax.ShapeDtypeStruct((per_device, rows, cells), f32)] * 2,
        in_specs=[vmem, vmem, vmem, pl.BlockSpec(memory_space=pl.ANY), pl.BlockSpec(memory_space=pltpu.SMEM)],
        out_specs=[vmem, vmem],
        scratch_shapes=[
            pltpu.VMEM((per_device, frames * modes), bf16),
            pltpu.VMEM((frames, modes, rows, cells), bf16),
            pltpu.VMEM((frames, rows, modes, cells), bf16),
            pltpu.VMEM((frames,) + block, bf16),
            pltpu.VMEM((frames,) + block, bf16),
            pltpu.VMEM((frames,) + block, bf16),
            pltpu.VMEM((frames,) + block, bf16),
            pltpu.VMEM((frames, 4, 256, LANES), f32),
            pltpu.VMEM(block, bf16),
            pltpu.VMEM(block, bf16),
            pltpu.VMEM(block, bf16),
            pltpu.VMEM(block, bf16),
            pltpu.VMEM((rows + 2, per_device, cells), bf16),
            dma((frames,)), dma(()), dma(()),
            dma((frames,)), dma((frames,)), dma((frames,)),
            dma((frames,)), dma((frames,)), dma((frames,)),
            dma(()), dma(()), dma(()),
            dma(()), dma(()), dma(()),
            dma((2,)), dma((2,)),
        ],
        compiler_params=pltpu.CompilerParams(
            collective_id=0, has_side_effects=True, vmem_limit_bytes=40 * 1024 * 1024
        ),
    )(coefficients.reshape(per_device, frames * modes), pick_own, pick_other, mode_basis, shift)
    return recon, sensor


def solution(mesh):
    placed = (P("query", None, None), P(None, None, "loop", None), P(), P())
    return jax.shard_map(
        shards,
        mesh=mesh,
        in_specs=placed,
        out_specs=(P("query", "loop", None), P("query", "loop", None)),
        check_vma=False,
    )
```

time: 225 us -> 72.6 us (0.32); the launches traced: 221 us -> 72.4 us
  waiting for transfers between devices: 103 us -> 0 us
  starting transfers between devices: 85.2 us -> 0 us
  Pallas kernels: 0 us -> 66.1 us
  other arithmetic: 15.6 us -> 2.33 us
  local copies, waits for them, and re-layouts: 9.63 us -> 3.31 us
  blocking collectives: 5.62 us -> 0 us
    ppermute x11 -> x0, waiting for transfers between devices: 103 us -> none  [the longest x9 102 us: shifted(): return lax.ppermute(value, axis, pairs)]
    ppermute x11 -> x0, starting transfers between devices: 85.2 us -> none  [the longest x9 56.9 us: shifted(): return lax.ppermute(value, axis, pairs)]
    pallas_call x0 -> x1, Pallas kernels: none -> 66.1 us  [shards(): pl.pallas_call(kernel, out_shape=[jax.ShapeDtypeStruct((per_device, rows,...]
    select_n x7 -> x1, other arithmetic: 10.5 us -> 0.08 us  [shards(): pick_other = jnp.where(group == 0, second, first)]
    all_gather x1 -> x0, blocking collectives: 5.62 us -> none  [shards(): gathered = lax.all_gather(coefficients, 'query', axis=0, tiled=True)]
    gather x4 -> x0, local copies, waits for them, and re-layouts: 4.5 us -> none  [single(): return lax.dynamic_slice_in_dim(block, begin, length, 0)]
    eq x8 -> x0, local copies, waits for them, and re-layouts: 3.32 us -> none  [shards(): taken = (coarse // distance % 2 == 1)[:, :, None, None]]
    unnamed x16 -> x6, local copies, waits for them, and re-layouts: 0.05 us -> 3.3 us
  transfers between devices with their start and end apart: 11 -> 0, of which waited for: 10 -> 0; matrix products, arithmetic and copies ran while one was open for 2% -> 0% of each run, Pallas kernels for 0% -> 0%
where the time goes in v1:
time: 72.6 us; the launch traced here: 72.4 us
  Pallas kernels  66.1 us (91%)
  local copies, waits for them, and re-layouts  3.31 us (5%)
  other arithmetic  2.33 us (3%)
    pallas_call x1, Pallas kernels, shards(): pl.pallas_call(kernel, out_shape=[jax.ShapeDtypeStruct((per_device, rows,...  66.1 us
    unnamed x6, local copies, waits for them, and re-layouts  3.3 us

profile of v1, /device:TPU:1, one launch (start us, length us, event | category | flops | bytes accessed | tf_op | source)
XLA Modules:
  0.0 72.4 jit_solution(15840455863131346119)
XLA Ops:
  0.6 0.0 copy-start
  0.7 0.7 broadcast_compare_fusion
  1.3 0.1 convert_reduce_fusion
  1.4 0.7 compare_and_fusion
  2.1 0.8 %select_reduce_fusion.shift = s32[3]{0:T(128)S(1)} fusion(s32[32,3]{0,1:T(4,128)} %param.6, pred[32]{0:T(512)(128)(4,1)S(1)} %compare_and_fusion), kind=kLoop, calls=%fused_computation.9 | loop fusion | flops 189 | bytes 428 | tf_op jit(solution)/shard_map/reduce_sum | solution.py:217
  2.9 0.1 broadcast_select_fusion
  3.0 0.0 copy-done
  3.0 0.0 copy-start.1
  3.0 1.9 %copy-done.1 = bf16[3,128,32,128]{3,2,1,0:T(8,128)(2,1)S(1)} copy-done((bf16[3,128,32,128]{3,2,1,0:T(8,128)(2,1)S(1)}, bf16[3,128,32,128]{3,2,1,0:T(8,128)(2,1)}, u32[]{:S(2)}) %copy-start.1) | copy-done | bytes 3145752
  4.9 66.1 %shard_map.59 = (f32[16,32,128]{2,1,0:T(8,128)S(1)}, f32[16,32,128]{2,1,0:T(8,128)S(1)}) custom-call(bf16[16,384]{1,0:T(8,128)(2,1)S(1)} %copy_bitcast_fusion.coef, bf16[16,16]{1,0:T(8,128)(2,1)S(1)} %get-tuple-element.3.pick_own, bf16[16,16]{1,0:T(8,128)(2,1)S(1)} %get-tuple-element.2.pick_other, bf16[3,128,32,128]{3,2,1,0:T(8,128)(2,1)S(1)} %copy-done.1, ...), custom_call_target="tpu_custom_call" | custom-call | tf_op jit(solution)/shard_map/pallas_call | solution.py:226
  71.0 0.7 copy.13
  71.7 0.7 copy.14
  (2 shorter events, 0.0 us)
Async XLA Ops:
  0.6 2.4 %copy-start = (bf16[16,3,128]{2,0,1:T(8,128)(2,1)S(1)}, bf16[16,3,128]{2,0,1:T(8,128)(2,1)}, u32[]{:S(2)}) copy-start(bf16[16,3,128]{2,0,1:T(8,128)(2,1)} %param.4) | copy-start | bytes 36868
  3.0 1.9 %copy-start.1 = (bf16[3,128,32,128]{3,2,1,0:T(8,128)(2,1)S(1)}, bf16[3,128,32,128]{3,2,1,0:T(8,128)(2,1)}, u32[]{:S(2)}) copy-start(bf16[3,128,32,128]{3,2,1,0:T(8,128)(2,1)} %basis.1) | copy-start | bytes 9437188

commit v2 on v1

v2 whole, which is shorter than its diff:
```python
import functools

import jax
import jax.numpy as jnp
from jax import lax
from jax.experimental import pallas as pl
from jax.experimental.pallas import tpu as pltpu
from jax.sharding import PartitionSpec as P

MESH = pl.DeviceIdType.MESH
RING = 16
LANES = 128
WIDE = 4
PARTS = 2


def swapped(tiles):
    lane = lax.broadcasted_iota(jnp.int32, tiles[0].shape, 1)
    count = len(tiles)
    step = 1
    while step < count:
        width = step * (LANES // count)
        low = (lane // width) % 2 == 0
        new = [None] * count
        for i in range(count):
            if i & step:
                continue
            a, b = tiles[i], tiles[i | step]
            new[i] = jnp.where(low, a, pltpu.roll(b, width, 1))
            new[i | step] = jnp.where(low, pltpu.roll(a, LANES - width, 1), b)
        tiles = new
        step = step * 2
    return tiles


def kernel(
    coef, basis, shifts, owners, field,
    shift_in, owner_in, owner_row, coefs, raw, modes, s1, r1, s2, r2, long, s3, r3, s4, r4,
    basis_sem, small_sem, coef_send, coef_recv, send1, recv1, own1, send2, recv2, own2,
    send3, recv3, own3, send4, recv4, own4, halo_send, halo_recv,
):
    me = lax.axis_index("loop")
    group = lax.axis_index("query")
    devices = lax.axis_size("loop")
    core = me % 2
    z = (me // 2) % RING
    sup = me // (2 * RING)
    spot = sup * 2 + core
    before = (me + devices - 1) % devices
    after = (me + 1) % devices

    def at_z(i):
        return sup * (2 * RING) + i * 2 + core

    def at_spot(i):
        return (i // 2) * (2 * RING) + z * 2 + i % 2

    barrier = pltpu.get_barrier_semaphore()

    def greet_z(k, carry):
        d = RING // 2 + (1 - 2 * (k % 2)) * ((k + 1) // 2)
        pl.semaphore_signal(barrier, inc=1, device_id={"loop": at_z((z + d) % RING)}, device_id_type=MESH)
        return carry

    def greet(d, carry):
        pl.semaphore_signal(barrier, inc=1, device_id={"loop": at_spot((spot + d) % RING)}, device_id_type=MESH)
        return carry

    lax.fori_loop(0, RING - 1, greet_z, 0)
    pl.semaphore_signal(barrier, inc=1, device_id={"query": 1 - group}, device_id_type=MESH)
    lax.fori_loop(1, RING, greet, 0)
    pl.semaphore_signal(barrier, inc=1, device_id={"loop": before}, device_id_type=MESH)
    pl.semaphore_signal(barrier, inc=1, device_id={"loop": after}, device_id_type=MESH)

    frames = basis.shape[0]
    mine_at = pl.ds(pl.multiple_of(group * RING, RING), RING)
    small = [
        pltpu.make_async_copy(owners, owner_row, small_sem.at[0]),
        pltpu.make_async_copy(coef, coefs.at[:, mine_at], small_sem.at[1]),
        pltpu.make_async_copy(owners, owner_in, small_sem.at[2]),
        pltpu.make_async_copy(shifts, shift_in, small_sem.at[3]),
    ]
    loads = [pltpu.make_async_copy(basis.at[f], raw.at[f], basis_sem.at[f]) for f in range(frames)]
    for load in small + loads:
        load.start()
    pl.semaphore_wait(barrier, 2 * (RING - 1) + 3)
    exchange = pltpu.make_async_remote_copy(
        src_ref=coef, dst_ref=coefs.at[:, mine_at], send_sem=coef_send, recv_sem=coef_recv,
        device_id={"query": 1 - group}, device_id_type=MESH,
    )
    exchange.start()

    def spread(source, target, here, to, send_sem, recv_sem, own_sem):
        pltpu.make_async_copy(source.at[here], target.at[here], own_sem).start()

        def one(d, carry):
            i = (here + d) % RING
            pltpu.make_async_remote_copy(
                src_ref=source.at[i], dst_ref=target.at[here], send_sem=send_sem, recv_sem=recv_sem,
                device_id={"loop": to(i)}, device_id_type=MESH,
            ).start()
            return carry

        lax.fori_loop(1, RING, one, 0)

    def landed(source, target, here, recv_sem, own_sem):
        pltpu.make_async_copy(source.at[here], target.at[here], own_sem).wait()
        most = target.at[pl.ds(0, RING - 1)]
        pltpu.make_async_copy(most, most, recv_sem).wait()

    def sent(source, send_sem):
        most = source.at[pl.ds(0, RING - 1)]
        pltpu.make_async_copy(most, most, send_sem).wait()

    queries = owners.shape[1]
    small[0].wait()
    mine = (owner_row[...] == group).astype(jnp.float32)
    mine = jnp.broadcast_to(mine, (RING, queries))
    row = lax.broadcasted_iota(jnp.int32, (queries, queries), 0)
    column = lax.broadcasted_iota(jnp.int32, (queries, queries), 1)
    triangle = (row < column).astype(jnp.bfloat16)
    rank = jnp.dot(mine.astype(jnp.bfloat16), triangle, preferred_element_type=jnp.float32)
    slot = lax.broadcasted_iota(jnp.int32, (RING, queries), 0).astype(jnp.float32)
    picked = jnp.where(rank == slot, mine, 0.0).astype(jnp.bfloat16)
    small[1].wait()

    def first(h, f):
        spread(s1.at[h, f], r1.at[h, f], z, at_z, send1.at[h, f], recv1.at[h, f], own1.at[h, f])

    for f in range(frames):
        loads[f].wait()
        modes[f] = jnp.swapaxes(raw[f], 0, 1)
        if f == 0:
            exchange.wait()
        weights = jnp.dot(picked, coefs[f], preferred_element_type=jnp.float32).astype(jnp.bfloat16)
        tiles = [
            jnp.dot(weights, modes[f, x], preferred_element_type=jnp.float32).astype(jnp.bfloat16)
            for x in range(2 * RING)
        ]
        tiles = swapped(tiles)
        for h in range(PARTS):
            for i in range(RING):
                s1[h, f, i] = tiles[h * RING + i]
        first(0, f)
    for f in range(frames):
        first(1, f)

    small[2].wait()
    small[3].wait()
    count = jnp.int32(0)
    cells_of = [jnp.int32(0)] * frames
    for q in range(queries):
        own = owner_in[0, q] == group
        here = jnp.logical_and(own, count == spot)
        cells_of = [jnp.where(here, shift_in[f, q], cells_of[f]) for f in range(frames)]
        count = count + own.astype(jnp.int32)

    def second(h):
        for f in range(frames):
            landed(s1.at[h, f], r1.at[h, f], z, recv1.at[h, f], own1.at[h, f])
            s2[h, f] = jnp.swapaxes(r1[h, f], 0, 1)
            spread(s2.at[h, f], r2.at[h, f], spot, at_spot, send2.at[h, f], recv2.at[h, f], own2.at[h, f])

    lane = lax.broadcasted_iota(jnp.int32, (128, LANES), 1)

    def third(h):
        for f in range(frames):
            landed(s2.at[h, f], r2.at[h, f], spot, recv2.at[h, f], own2.at[h, f])
            for i in range(RING):
                part = r2[h, f, i].astype(jnp.float32)
                at = (i // 2) * RING
                long[h, f, i % 2, at:at + RING] = part
                long[h, f, i % 2, 128 + at:128 + at + RING] = part
        for j in range(2):
            total = None
            for f in range(frames):
                rows = cells_of[f] // 32
                turn = (cells_of[f] % 32) * WIDE

                def moved(rows):
                    low = rows % 2
                    down = (rows // 2 + (j < low).astype(jnp.int32)) % 128
                    return long[h, f, (j + 2 - low) % 2, pl.ds(128 - down, 128), :]

                both = jnp.where(lane >= LANES - turn, moved(rows + 1), moved(rows))
                both = pltpu.roll(both, turn, 1)
                total = both if total is None else total + both
            total = total.astype(jnp.bfloat16)
            for i in range(8):
                s3[h, i * 2 + j] = total[i * RING:(i + 1) * RING]
        spread(s3.at[h], r3.at[h], spot, at_spot, send3.at[h], recv3.at[h], own3.at[h])

    def fourth(h):
        landed(s3.at[h], r3.at[h], spot, recv3.at[h], own3.at[h])
        s4[h] = jnp.swapaxes(r3[h], 0, 1)
        spread(s4.at[h], r4.at[h], z, at_z, send4.at[h], recv4.at[h], own4.at[h])

    second(0)
    third(0)
    second(1)
    fourth(0)
    third(1)
    fourth(1)
    for h in range(PARTS):
        landed(s4.at[h], r4.at[h], z, recv4.at[h], own4.at[h])
    tiles = swapped([r4[h, i] for h in range(PARTS) for i in range(RING)])
    for x in range(2 * RING):
        field[1 + x] = tiles[x]

    length = 2 * RING
    up = pltpu.make_async_remote_copy(
        src_ref=field.at[length], dst_ref=field.at[0], send_sem=halo_send.at[0], recv_sem=halo_recv.at[0],
        device_id={"loop": after}, device_id_type=MESH,
    )
    down = pltpu.make_async_remote_copy(
        src_ref=field.at[1], dst_ref=field.at[length + 1], send_sem=halo_send.at[1], recv_sem=halo_recv.at[1],
        device_id={"loop": before}, device_id_type=MESH,
    )
    up.start()
    down.start()
    for h in range(PARTS):
        for f in range(frames):
            sent(s1.at[h, f], send1.at[h, f])
            sent(s2.at[h, f], send2.at[h, f])
        sent(s3.at[h], send3.at[h])
        sent(s4.at[h], send4.at[h])
    up.wait()
    down.wait()


def finish(field, recon, sensor):
    u = field[...].astype(jnp.float32)
    center, upper, lower = u[1:-1], u[2:], u[:-2]
    recon[...] = jnp.swapaxes(center, 0, 1)
    place = lax.broadcasted_iota(jnp.int32, center.shape, 2)
    right = jnp.where(place == LANES - 1, 0.0, pltpu.roll(center, LANES - 1, 2))
    left = jnp.where(place == 0, 0.0, pltpu.roll(center, 1, 2))
    numerator = jnp.abs(upper - 2.0 * center + lower) + jnp.abs(right - 2.0 * center + left)
    denominator = jnp.maximum(jnp.abs(upper) + 2.0 * jnp.abs(center) + jnp.abs(lower), 1.0)
    sensor[...] = jnp.swapaxes(numerator / denominator, 0, 1)


def shards(coefficients, mode_basis, shifts, owners):
    per_device = coefficients.shape[0]
    queries = owners.shape[0]
    frames, modes, rows, cells = mode_basis.shape
    bf16, f32 = jnp.bfloat16, jnp.float32
    block = (RING, RING, LANES)
    hbm = pl.BlockSpec(memory_space=pltpu.HBM)
    dma = pltpu.SemaphoreType.DMA
    field = pl.pallas_call(
        kernel,
        out_shape=jax.ShapeDtypeStruct((rows + 2, per_device, cells), bf16),
        in_specs=[hbm, hbm, hbm, hbm],
        out_specs=pl.BlockSpec(memory_space=pltpu.VMEM),
        scratch_shapes=[
            pltpu.SMEM((frames, queries), jnp.int32),
            pltpu.SMEM((1, queries), jnp.int32),
            pltpu.VMEM((1, queries), jnp.int32),
            pltpu.VMEM((frames, queries, modes), bf16),
            pltpu.VMEM((frames, modes, rows, cells), bf16),
            pltpu.VMEM((frames, rows, modes, cells), bf16),
            pltpu.VMEM((PARTS, frames) + block, bf16),
            pltpu.VMEM((PARTS, frames) + block, bf16),
            pltpu.VMEM((PARTS, frames) + block, bf16),
            pltpu.VMEM((PARTS, frames) + block, bf16),
            pltpu.VMEM((PARTS, frames, 2, 256, LANES), f32),
            pltpu.VMEM((PARTS,) + block, bf16),
            pltpu.VMEM((PARTS,) + block, bf16),
            pltpu.VMEM((PARTS,) + block, bf16),
            pltpu.VMEM((PARTS,) + block, bf16),
            dma((frames,)), dma((4,)), dma(()), dma(()),
            dma((PARTS, frames)), dma((PARTS, frames)), dma((PARTS, frames)),
            dma((PARTS, frames)), dma((PARTS, frames)), dma((PARTS, frames)),
            dma((PARTS,)), dma((PARTS,)), dma((PARTS,)),
            dma((PARTS,)), dma((PARTS,)), dma((PARTS,)),
            dma((2,)), dma((2,)),
        ],
        compiler_params=pltpu.CompilerParams(
            collective_id=0, has_side_effects=True, vmem_limit_bytes=63 * 1024 * 1024
        ),
    )(jnp.swapaxes(coefficients, 0, 1), mode_basis, shifts.T, owners.reshape(1, queries))
    part = 8
    out = pl.BlockSpec((part, rows, cells), lambda i: (i, 0, 0))
    recon, sensor = pl.pallas_call(
        finish,
        grid=(per_device // part,),
        out_shape=[jax.ShapeDtypeStruct((per_device, rows, cells), f32)] * 2,
        in_specs=[pl.BlockSpec((rows + 2, part, cells), lambda i: (0, i, 0))],
        out_specs=[out, out],
        compiler_params=pltpu.CompilerParams(vmem_limit_bytes=63 * 1024 * 1024),
    )(field)
    return recon, sensor


def solution(mesh):
    placed = (P("query", None, None), P(None, None, "loop", None), P(), P())
    return jax.shard_map(
        shards,
        mesh=mesh,
        in_specs=placed,
        out_specs=(P("query", "loop", None), P("query", "loop", None)),
        check_vma=False,
    )
```

time: 72.6 us -> 66.7 us (0.919)
  local copies, waits for them, and re-layouts: 3.31 us -> 0 us
  other arithmetic: 2.33 us -> 0 us
    unnamed x6 -> x0, local copies, waits for them, and re-layouts: 3.3 us -> none
    reduce_sum x2 -> x0, other arithmetic: 0.91 us -> none  [the longest x1 0.8 us: shards(): jnp.sum(jnp.where((mine & (rank == spot))[:, None], shifts, 0), axis=0)]
    pallas_call x1 -> x2, Pallas kernels: 66.1 us -> 65.9 us  [the longest x1 64 us: shards(): pl.pallas_call(kernel, out_shape=jax.ShapeDtypeStruct((rows + 2, per_devi...]
where the time goes in v2:
time: 66.7 us; the launch traced here: 66.5 us
  Pallas kernels  65.9 us (99%)
    pallas_call x1, Pallas kernels, shards(): pl.pallas_call(kernel, out_shape=jax.ShapeDtypeStruct((rows + 2, per_devi...  64 us
    pallas_call x1, Pallas kernels, shards(): pl.pallas_call(finish, grid=(per_device // part,), out_shape=[jax.ShapeDt...  1.88 us

profile of v2, /device:TPU:1, one launch (start us, length us, event | category | flops | bytes accessed | tf_op | source)
XLA Modules:
  0.0 66.5 jit_solution(18165499237015098010)
XLA Ops:
  0.6 64.0 %shard_map.59.field = bf16[34,16,128]{2,1,0:T(8,128)(2,1)} custom-call(bf16[3,16,128]{2,1,0:T(8,128)(2,1)} %bitcast.3, bf16[3,128,32,128]{3,2,1,0:T(8,128)(2,1)} %basis.1, s32[3,32]{1,0:T(4,128)} %bitcast.4, s32[1,32]{1,0:T(1,128)} %bitcast.5), custom_call_target="tpu_custom_call" | custom-call | tf_op jit(solution)/shard_map/pallas_call | solution.py:251
  64.6 1.9 %shard_map.60 = (f32[16,32,128]{2,1,0:T(8,128)}, f32[16,32,128]{2,1,0:T(8,128)}) custom-call(bf16[34,16,128]{2,1,0:T(8,128)(2,1)} %shard_map.59.field), custom_call_target="tpu_custom_call" | custom-call | tf_op jit(solution)/shard_map/pallas_call | solution.py:285

commit v3 on v2

--- a/solution.py
+++ b/solution.py
@@ -35,8 +35,8 @@
 
 def kernel(
     coef, basis, shifts, owners, field,
-    shift_in, owner_in, owner_row, coefs, raw, modes, s1, r1, s2, r2, long, s3, r3, s4, r4,
-    basis_sem, small_sem, coef_send, coef_recv, send1, recv1, own1, send2, recv2, own2,
+    shift_in, owner_row, coefs, raw, modes, s1, r1, s2, r2, long, s3, r3, s4, r4,
+    basis_sem, small_sem, send1, recv1, own1, send2, recv2, own2,
     send3, recv3, own3, send4, recv4, own4, halo_send, halo_recv,
 ):
     me = lax.axis_index("loop")
@@ -55,53 +55,54 @@
     def at_spot(i):
         return (i // 2) * (2 * RING) + z * 2 + i % 2
 
+    plane = 2 * RING
+    seat = group * RING + spot
+
+    def in_plane(i):
+        return {"loop": at_spot(i % RING), "query": i // RING}
+
+    def farthest_first(k):
+        return RING // 2 + (1 - 2 * (k % 2)) * ((k + 1) // 2)
+
     barrier = pltpu.get_barrier_semaphore()
 
     def greet_z(k, carry):
-        d = RING // 2 + (1 - 2 * (k % 2)) * ((k + 1) // 2)
-        pl.semaphore_signal(barrier, inc=1, device_id={"loop": at_z((z + d) % RING)}, device_id_type=MESH)
+        i = (z + farthest_first(k)) % RING
+        pl.semaphore_signal(barrier, inc=1, device_id={"loop": at_z(i)}, device_id_type=MESH)
         return carry
 
-    def greet(d, carry):
-        pl.semaphore_signal(barrier, inc=1, device_id={"loop": at_spot((spot + d) % RING)}, device_id_type=MESH)
+    def greet_plane(d, carry):
+        pl.semaphore_signal(barrier, inc=1, device_id=in_plane((seat + d) % plane), device_id_type=MESH)
         return carry
 
     lax.fori_loop(0, RING - 1, greet_z, 0)
-    pl.semaphore_signal(barrier, inc=1, device_id={"query": 1 - group}, device_id_type=MESH)
-    lax.fori_loop(1, RING, greet, 0)
+    lax.fori_loop(1, plane, greet_plane, 0)
     pl.semaphore_signal(barrier, inc=1, device_id={"loop": before}, device_id_type=MESH)
     pl.semaphore_signal(barrier, inc=1, device_id={"loop": after}, device_id_type=MESH)
 
     frames = basis.shape[0]
-    mine_at = pl.ds(pl.multiple_of(group * RING, RING), RING)
     small = [
-        pltpu.make_async_copy(owners, owner_row, small_sem.at[0]),
-        pltpu.make_async_copy(coef, coefs.at[:, mine_at], small_sem.at[1]),
-        pltpu.make_async_copy(owners, owner_in, small_sem.at[2]),
-        pltpu.make_async_copy(shifts, shift_in, small_sem.at[3]),
+        pltpu.make_async_copy(coef, coefs, small_sem.at[0]),
+        pltpu.make_async_copy(owners, owner_row, small_sem.at[1]),
+        pltpu.make_async_copy(shifts, shift_in, small_sem.at[2]),
     ]
     loads = [pltpu.make_async_copy(basis.at[f], raw.at[f], basis_sem.at[f]) for f in range(frames)]
-    for load in small + loads:
+    loads[0].start()
+    for load in small + loads[1:]:
         load.start()
-    pl.semaphore_wait(barrier, 2 * (RING - 1) + 3)
-    exchange = pltpu.make_async_remote_copy(
-        src_ref=coef, dst_ref=coefs.at[:, mine_at], send_sem=coef_send, recv_sem=coef_recv,
-        device_id={"query": 1 - group}, device_id_type=MESH,
-    )
-    exchange.start()
 
     def spread(source, target, here, to, send_sem, recv_sem, own_sem):
         pltpu.make_async_copy(source.at[here], target.at[here], own_sem).start()
 
-        def one(d, carry):
-            i = (here + d) % RING
+        def one(k, carry):
+            i = (here + farthest_first(k)) % RING
             pltpu.make_async_remote_copy(
                 src_ref=source.at[i], dst_ref=target.at[here], send_sem=send_sem, recv_sem=recv_sem,
                 device_id={"loop": to(i)}, device_id_type=MESH,
             ).start()
             return carry
 
-        lax.fori_loop(1, RING, one, 0)
+        lax.fori_loop(0, RING - 1, one, 0)
 
     def landed(source, target, here, recv_sem, own_sem):
         pltpu.make_async_copy(source.at[here], target.at[here], own_sem).wait()
@@ -112,18 +113,6 @@
         most = source.at[pl.ds(0, RING - 1)]
         pltpu.make_async_copy(most, most, send_sem).wait()
 
-    queries = owners.shape[1]
-    small[0].wait()
-    mine = (owner_row[...] == group).astype(jnp.float32)
-    mine = jnp.broadcast_to(mine, (RING, queries))
-    row = lax.broadcasted_iota(jnp.int32, (queries, queries), 0)
-    column = lax.broadcasted_iota(jnp.int32, (queries, queries), 1)
-    triangle = (row < column).astype(jnp.bfloat16)
-    rank = jnp.dot(mine.astype(jnp.bfloat16), triangle, preferred_element_type=jnp.float32)
-    slot = lax.broadcasted_iota(jnp.int32, (RING, queries), 0).astype(jnp.float32)
-    picked = jnp.where(rank == slot, mine, 0.0).astype(jnp.bfloat16)
-    small[1].wait()
-
     def first(h, f):
         spread(s1.at[h, f], r1.at[h, f], z, at_z, send1.at[h, f], recv1.at[h, f], own1.at[h, f])
 
@@ -131,8 +120,8 @@
         loads[f].wait()
         modes[f] = jnp.swapaxes(raw[f], 0, 1)
         if f == 0:
-            exchange.wait()
-        weights = jnp.dot(picked, coefs[f], preferred_element_type=jnp.float32).astype(jnp.bfloat16)
+            small[0].wait()
+        weights = coefs[f]
         tiles = [
             jnp.dot(weights, modes[f, x], preferred_element_type=jnp.float32).astype(jnp.bfloat16)
             for x in range(2 * RING)
@@ -141,19 +130,23 @@
         for h in range(PARTS):
             for i in range(RING):
                 s1[h, f, i] = tiles[h * RING + i]
+        if f == 0:
+            pl.semaphore_wait(barrier, RING - 1 + plane - 1 + 2)
         first(0, f)
     for f in range(frames):
         first(1, f)
 
+    queries = owners.shape[1]
+    small[1].wait()
     small[2].wait()
-    small[3].wait()
-    count = jnp.int32(0)
-    cells_of = [jnp.int32(0)] * frames
-    for q in range(queries):
-        own = owner_in[0, q] == group
-        here = jnp.logical_and(own, count == spot)
-        cells_of = [jnp.where(here, shift_in[f, q], cells_of[f]) for f in range(frames)]
-        count = count + own.astype(jnp.int32)
+    mine = jnp.broadcast_to((owner_row[...] == group).astype(jnp.float32), (RING, queries))
+    row = lax.broadcasted_iota(jnp.int32, (queries, queries), 0)
+    column = lax.broadcasted_iota(jnp.int32, (queries, queries), 1)
+    triangle = (row < column).astype(jnp.bfloat16)
+    rank = jnp.dot(mine.astype(jnp.bfloat16), triangle, preferred_element_type=jnp.float32)
+    slot = lax.broadcasted_iota(jnp.int32, (RING, queries), 0).astype(jnp.float32)
+    picked = jnp.where(rank == slot, mine, 0.0).astype(jnp.bfloat16)
+    cells_of = [shift_in[f, seat] for f in range(frames)]
 
     def second(h):
         for f in range(frames):
@@ -188,11 +181,25 @@
             total = total.astype(jnp.bfloat16)
             for i in range(8):
                 s3[h, i * 2 + j] = total[i * RING:(i + 1) * RING]
-        spread(s3.at[h], r3.at[h], spot, at_spot, send3.at[h], recv3.at[h], own3.at[h])
+        pltpu.make_async_copy(s3.at[h, spot], r3.at[h, seat], own3.at[h]).start()
+
+        def one(d, carry):
+            i = (seat + d) % plane
+            pltpu.make_async_remote_copy(
+                src_ref=s3.at[h, i % RING], dst_ref=r3.at[h, seat], send_sem=send3.at[h], recv_sem=recv3.at[h],
+                device_id=in_plane(i), device_id_type=MESH,
+            ).start()
+            return carry
+
+        lax.fori_loop(1, plane, one, 0)
 
     def fourth(h):
-        landed(s3.at[h], r3.at[h], spot, recv3.at[h], own3.at[h])
-        s4[h] = jnp.swapaxes(r3[h], 0, 1)
+        pltpu.make_async_copy(s3.at[h, spot], r3.at[h, seat], own3.at[h]).wait()
+        most = r3.at[h, pl.ds(0, plane - 1)]
+        pltpu.make_async_copy(most, most, recv3.at[h]).wait()
+        sums = jnp.swapaxes(r3[h], 0, 1)
+        for i in range(RING):
+            s4[h, i] = jnp.dot(picked, sums[i], preferred_element_type=jnp.float32).astype(jnp.bfloat16)
         spread(s4.at[h], r4.at[h], z, at_z, send4.at[h], recv4.at[h], own4.at[h])
 
     second(0)
@@ -222,7 +229,8 @@
         for f in range(frames):
             sent(s1.at[h, f], send1.at[h, f])
             sent(s2.at[h, f], send2.at[h, f])
-        sent(s3.at[h], send3.at[h])
+        most = r3.at[h, pl.ds(0, plane - 1)]
+        pltpu.make_async_copy(most, most, send3.at[h]).wait()
         sent(s4.at[h], send4.at[h])
     up.wait()
     down.wait()
@@ -255,9 +263,8 @@
         out_specs=pl.BlockSpec(memory_space=pltpu.VMEM),
         scratch_shapes=[
             pltpu.SMEM((frames, queries), jnp.int32),
-            pltpu.SMEM((1, queries), jnp.int32),
             pltpu.VMEM((1, queries), jnp.int32),
-            pltpu.VMEM((frames, queries, modes), bf16),
+            pltpu.VMEM((frames, per_device, modes), bf16),
             pltpu.VMEM((frames, modes, rows, cells), bf16),
             pltpu.VMEM((frames, rows, modes, cells), bf16),
             pltpu.VMEM((PARTS, frames) + block, bf16),
@@ -266,10 +273,10 @@
             pltpu.VMEM((PARTS, frames) + block, bf16),
             pltpu.VMEM((PARTS, frames, 2, 256, LANES), f32),
             pltpu.VMEM((PARTS,) + block, bf16),
+            pltpu.VMEM((PARTS, 2 * RING, RING, LANES), bf16),
             pltpu.VMEM((PARTS,) + block, bf16),
             pltpu.VMEM((PARTS,) + block, bf16),
-            pltpu.VMEM((PARTS,) + block, bf16),
-            dma((frames,)), dma((4,)), dma(()), dma(()),
+            dma((frames,)), dma((3,)),
             dma((PARTS, frames)), dma((PARTS, frames)), dma((PARTS, frames)),
             dma((PARTS, frames)), dma((PARTS, frames)), dma((PARTS, frames)),
             dma((PARTS,)), dma((PARTS,)), dma((PARTS,)),

time: 66.7 us -> 62.8 us (0.942)
  Pallas kernels: 65.9 us -> 62 us
    pallas_call x1, Pallas kernels: 64 us -> 60.1 us  [shards(): pl.pallas_call(kernel, out_shape=jax.ShapeDtypeStruct((rows + 2, per_devi...]
where the time goes in v3:
time: 62.8 us; the launch traced here: 62.7 us
  Pallas kernels  62 us (99%)
  between operations  0.64 us (1%)
    pallas_call x1, Pallas kernels, shards(): pl.pallas_call(kernel, out_shape=jax.ShapeDtypeStruct((rows + 2, per_devi...  60.1 us
    pallas_call x1, Pallas kernels, shards(): pl.pallas_call(finish, grid=(per_device // part,), out_shape=[jax.ShapeDt...  1.88 us

profile of v3, /device:TPU:1, one launch (start us, length us, event | category | flops | bytes accessed | tf_op | source)
XLA Modules:
  0.0 62.7 jit_solution(9438262380932571277)
XLA Ops:
  0.6 60.1 %shard_map.59.field = bf16[34,16,128]{2,1,0:T(8,128)(2,1)} custom-call(bf16[3,16,128]{2,1,0:T(8,128)(2,1)} %bitcast.3, bf16[3,128,32,128]{3,2,1,0:T(8,128)(2,1)} %basis.1, s32[3,32]{1,0:T(4,128)} %bitcast.4, s32[1,32]{1,0:T(1,128)} %bitcast.5), custom_call_target="tpu_custom_call" | custom-call | tf_op jit(solution)/shard_map/pallas_call | solution.py:259
  60.8 1.9 %shard_map.60 = (f32[16,32,128]{2,1,0:T(8,128)}, f32[16,32,128]{2,1,0:T(8,128)}) custom-call(bf16[34,16,128]{2,1,0:T(8,128)(2,1)} %shard_map.59.field), custom_call_target="tpu_custom_call" | custom-call | tf_op jit(solution)/shard_map/pallas_call | solution.py:292

commit v4 on v3

--- a/solution.py
+++ b/solution.py
@@ -35,8 +35,9 @@
 
 def kernel(
     coef, basis, shifts, owners, field,
-    shift_in, owner_row, coefs, raw, modes, s1, r1, s2, r2, long, s3, r3, s4, r4,
-    basis_sem, small_sem, send1, recv1, own1, send2, recv2, own2,
+    rows_in, shift_in, owner_row, coefs, raw, modes, s1, r1, s2, r2, long, s3, r3, s4, r4,
+    p1, q1, p2, q2, p3, q3, p4, q4,
+    basis_sem, small_sem, field_sem, send1, recv1, own1, send2, recv2, own2,
     send3, recv3, own3, send4, recv4, own4, halo_send, halo_recv,
 ):
     me = lax.axis_index("loop")
@@ -116,6 +117,29 @@
     def first(h, f):
         spread(s1.at[h, f], r1.at[h, f], z, at_z, send1.at[h, f], recv1.at[h, f], own1.at[h, f])
 
+    def spread_plane(source, target, send_sem, recv_sem, own_sem):
+        pltpu.make_async_copy(source.at[spot], target.at[seat], own_sem).start()
+
+        def one(d, carry):
+            i = (seat + d) % plane
+            pltpu.make_async_remote_copy(
+                src_ref=source.at[i % RING], dst_ref=target.at[seat], send_sem=send_sem, recv_sem=recv_sem,
+                device_id=in_plane(i), device_id_type=MESH,
+            ).start()
+            return carry
+
+        lax.fori_loop(1, plane, one, 0)
+
+    def landed_plane(source, target, recv_sem, own_sem):
+        pltpu.make_async_copy(source.at[spot], target.at[seat], own_sem).wait()
+        most = target.at[pl.ds(0, plane - 1)]
+        pltpu.make_async_copy(most, most, recv_sem).wait()
+
+    def sent_plane(target, send_sem):
+        most = target.at[pl.ds(0, plane - 1)]
+        pltpu.make_async_copy(most, most, send_sem).wait()
+
+    last = frames
     for f in range(frames):
         loads[f].wait()
         modes[f] = jnp.swapaxes(raw[f], 0, 1)
@@ -127,14 +151,13 @@
             for x in range(2 * RING)
         ]
         tiles = swapped(tiles)
-        for h in range(PARTS):
-            for i in range(RING):
-                s1[h, f, i] = tiles[h * RING + i]
+        for i in range(RING):
+            s1[f, i] = tiles[i]
         if f == 0:
             pl.semaphore_wait(barrier, RING - 1 + plane - 1 + 2)
-        first(0, f)
-    for f in range(frames):
-        first(1, f)
+        spread(s1.at[f], r1.at[f], z, at_z, send1.at[f], recv1.at[f], own1.at[f])
+        p1[:, f] = jnp.swapaxes(jnp.stack(tiles[RING:]), 0, 1)
+    spread(p1, q1, spot, at_spot, send2.at[last], recv2.at[last], own2.at[last])
 
     queries = owners.shape[1]
     small[1].wait()
@@ -148,22 +171,16 @@
     picked = jnp.where(rank == slot, mine, 0.0).astype(jnp.bfloat16)
     cells_of = [shift_in[f, seat] for f in range(frames)]
 
-    def second(h):
-        for f in range(frames):
-            landed(s1.at[h, f], r1.at[h, f], z, recv1.at[h, f], own1.at[h, f])
-            s2[h, f] = jnp.swapaxes(r1[h, f], 0, 1)
-            spread(s2.at[h, f], r2.at[h, f], spot, at_spot, send2.at[h, f], recv2.at[h, f], own2.at[h, f])
-
     lane = lax.broadcasted_iota(jnp.int32, (128, LANES), 1)
 
-    def third(h):
-        for f in range(frames):
-            landed(s2.at[h, f], r2.at[h, f], spot, recv2.at[h, f], own2.at[h, f])
-            for i in range(RING):
-                part = r2[h, f, i].astype(jnp.float32)
-                at = (i // 2) * RING
-                long[h, f, i % 2, at:at + RING] = part
-                long[h, f, i % 2, 128 + at:128 + at + RING] = part
+    def store_long(h, f, i, part):
+        part = part.astype(jnp.float32)
+        at = (i // 2) * RING
+        long[h, f, i % 2, at:at + RING] = part
+        long[h, f, i % 2, 128 + at:128 + at + RING] = part
+
+    def summed(h):
+        sums = []
         for j in range(2):
             total = None
             for f in range(frames):
@@ -178,60 +195,81 @@
                 both = jnp.where(lane >= LANES - turn, moved(rows + 1), moved(rows))
                 both = pltpu.roll(both, turn, 1)
                 total = both if total is None else total + both
-            total = total.astype(jnp.bfloat16)
-            for i in range(8):
-                s3[h, i * 2 + j] = total[i * RING:(i + 1) * RING]
-        pltpu.make_async_copy(s3.at[h, spot], r3.at[h, seat], own3.at[h]).start()
-
-        def one(d, carry):
-            i = (seat + d) % plane
-            pltpu.make_async_remote_copy(
-                src_ref=s3.at[h, i % RING], dst_ref=r3.at[h, seat], send_sem=send3.at[h], recv_sem=recv3.at[h],
-                device_id=in_plane(i), device_id_type=MESH,
-            ).start()
-            return carry
-
-        lax.fori_loop(1, plane, one, 0)
-
-    def fourth(h):
-        pltpu.make_async_copy(s3.at[h, spot], r3.at[h, seat], own3.at[h]).wait()
-        most = r3.at[h, pl.ds(0, plane - 1)]
-        pltpu.make_async_copy(most, most, recv3.at[h]).wait()
-        sums = jnp.swapaxes(r3[h], 0, 1)
+            sums.append(total.astype(jnp.bfloat16))
+        return [sums[i % 2][(i // 2) * RING:(i // 2 + 1) * RING] for i in range(RING)]
+
+    def owned(blocks):
+        blocks = jnp.swapaxes(blocks, 0, 1)
+        return [
+            jnp.dot(picked, blocks[i], preferred_element_type=jnp.float32).astype(jnp.bfloat16)
+            for i in range(RING)
+        ]
+
+    landed(p1, q1, spot, recv2.at[last], own2.at[last])
+    for f in range(frames):
+        p2[:, f] = jnp.swapaxes(q1[:, f], 0, 1)
+    spread(p2, q2, z, at_z, send1.at[last], recv1.at[last], own1.at[last])
+
+    for f in range(frames):
+        landed(s1.at[f], r1.at[f], z, recv1.at[f], own1.at[f])
+        s2[f] = jnp.swapaxes(r1[f], 0, 1)
+        spread(s2.at[f], r2.at[f], spot, at_spot, send2.at[f], recv2.at[f], own2.at[f])
+    for f in range(frames):
+        landed(s2.at[f], r2.at[f], spot, recv2.at[f], own2.at[f])
         for i in range(RING):
-            s4[h, i] = jnp.dot(picked, sums[i], preferred_element_type=jnp.float32).astype(jnp.bfloat16)
-        spread(s4.at[h], r4.at[h], z, at_z, send4.at[h], recv4.at[h], own4.at[h])
-
-    second(0)
-    third(0)
-    second(1)
-    fourth(0)
-    third(1)
-    fourth(1)
-    for h in range(PARTS):
-        landed(s4.at[h], r4.at[h], z, recv4.at[h], own4.at[h])
-    tiles = swapped([r4[h, i] for h in range(PARTS) for i in range(RING)])
+            store_long(0, f, i, r2[f, i])
+    parts = summed(0)
+    for i in range(RING):
+        s3[i] = parts[i]
+    spread_plane(s3, r3, send3.at[0], recv3.at[0], own3.at[0])
+
+    landed(p2, q2, z, recv1.at[last], own1.at[last])
+    for f in range(frames):
+        blocks = jnp.swapaxes(q2[:, f], 0, 1)
+        for i in range(RING):
+            store_long(1, f, i, blocks[i])
+    p3[...] = jnp.swapaxes(jnp.stack(summed(1)), 0, 1)
+    spread(p3, q3, z, at_z, send4.at[1], recv4.at[1], own4.at[1])
+
+    landed_plane(s3, r3, recv3.at[0], own3.at[0])
+    parts = owned(r3[...])
+    for i in range(RING):
+        s4[i] = parts[i]
+    spread(s4, r4, z, at_z, send4.at[0], recv4.at[0], own4.at[0])
+
+    landed(p3, q3, z, recv4.at[1], own4.at[1])
+    p4[...] = jnp.swapaxes(q3[...], 0, 1)
+    spread_plane(p4, q4, send3.at[1], recv3.at[1], own3.at[1])
+
+    landed(s4, r4, z, recv4.at[0], own4.at[0])
+    landed_plane(p4, q4, recv3.at[1], own3.at[1])
+    tiles = swapped([r4[i] for i in range(RING)] + owned(q4[...]))
     for x in range(2 * RING):
-        field[1 + x] = tiles[x]
+        rows_in[x] = tiles[x]
 
     length = 2 * RING
     up = pltpu.make_async_remote_copy(
-        src_ref=field.at[length], dst_ref=field.at[0], send_sem=halo_send.at[0], recv_sem=halo_recv.at[0],
+        src_ref=rows_in.at[length - 1], dst_ref=field.at[0], send_sem=halo_send.at[0], recv_sem=halo_recv.at[0],
         device_id={"loop": after}, device_id_type=MESH,
     )
     down = pltpu.make_async_remote_copy(
-        src_ref=field.at[1], dst_ref=field.at[length + 1], send_sem=halo_send.at[1], recv_sem=halo_recv.at[1],
+        src_ref=rows_in.at[0], dst_ref=field.at[length + 1], send_sem=halo_send.at[1], recv_sem=halo_recv.at[1],
         device_id={"loop": before}, device_id_type=MESH,
     )
     up.start()
     down.start()
-    for h in range(PARTS):
-        for f in range(frames):
-            sent(s1.at[h, f], send1.at[h, f])
-            sent(s2.at[h, f], send2.at[h, f])
-        most = r3.at[h, pl.ds(0, plane - 1)]
-        pltpu.make_async_copy(most, most, send3.at[h]).wait()
-        sent(s4.at[h], send4.at[h])
+    inside = pltpu.make_async_copy(rows_in, field.at[pl.ds(1, length)], field_sem)
+    inside.start()
+    for f in range(frames):
+        sent(s1.at[f], send1.at[f])
+        sent(s2.at[f], send2.at[f])
+    sent(p1, send2.at[last])
+    sent(p2, send1.at[last])
+    sent_plane(r3, send3.at[0])
+    sent(s4, send4.at[0])
+    sent(p3, send4.at[1])
+    sent_plane(q4, send3.at[1])
+    inside.wait()
     up.wait()
     down.wait()
 
@@ -260,25 +298,34 @@
         kernel,
         out_shape=jax.ShapeDtypeStruct((rows + 2, per_device, cells), bf16),
         in_specs=[hbm, hbm, hbm, hbm],
-        out_specs=pl.BlockSpec(memory_space=pltpu.VMEM),
+        out_specs=hbm,
         scratch_shapes=[
+            pltpu.VMEM((rows, per_device, cells), bf16),
             pltpu.SMEM((frames, queries), jnp.int32),
             pltpu.VMEM((1, queries), jnp.int32),
             pltpu.VMEM((frames, per_device, modes), bf16),
             pltpu.VMEM((frames, modes, rows, cells), bf16),
             pltpu.VMEM((frames, rows, modes, cells), bf16),
-            pltpu.VMEM((PARTS, frames) + block, bf16),
-            pltpu.VMEM((PARTS, frames) + block, bf16),
-            pltpu.VMEM((PARTS, frames) + block, bf16),
-            pltpu.VMEM((PARTS, frames) + block, bf16),
+            pltpu.VMEM((frames,) + block, bf16),
+            pltpu.VMEM((frames,) + block, bf16),
+            pltpu.VMEM((frames,) + block, bf16),
+            pltpu.VMEM((frames,) + block, bf16),
             pltpu.VMEM((PARTS, frames, 2, 256, LANES), f32),
-            pltpu.VMEM((PARTS,) + block, bf16),
-            pltpu.VMEM((PARTS, 2 * RING, RING, LANES), bf16),
-            pltpu.VMEM((PARTS,) + block, bf16),
-            pltpu.VMEM((PARTS,) + block, bf16),
-            dma((frames,)), dma((3,)),
-            dma((PARTS, frames)), dma((PARTS, frames)), dma((PARTS, frames)),
-            dma((PARTS, frames)), dma((PARTS, frames)), dma((PARTS, frames)),
+            pltpu.VMEM(block, bf16),
+            pltpu.VMEM((2 * RING, RING, LANES), bf16),
+            pltpu.VMEM(block, bf16),
+            pltpu.VMEM(block, bf16),
+            pltpu.VMEM((RING, frames, RING, LANES), bf16),
+            pltpu.VMEM((RING, frames, RING, LANES), bf16),
+            pltpu.VMEM((RING, frames, RING, LANES), bf16),
+            pltpu.VMEM((RING, frames, RING, LANES), bf16),
+            pltpu.VMEM(block, bf16),
+            pltpu.VMEM(block, bf16),
+            pltpu.VMEM(block, bf16),
+            pltpu.VMEM((2 * RING, RING, LANES), bf16),
+            dma((frames,)), dma((3,)), dma(()),
+            dma((frames + 1,)), dma((frames + 1,)), dma((frames + 1,)),
+            dma((frames + 1,)), dma((frames + 1,)), dma((frames + 1,)),
             dma((PARTS,)), dma((PARTS,)), dma((PARTS,)),
             dma((PARTS,)), dma((PARTS,)), dma((PARTS,)),
             dma((2,)), dma((2,)),

time: 62.8 us -> 56.4 us (0.90); the launches traced: 62.7 us -> 55.6 us
  Pallas kernels: 62 us -> 55 us
    pallas_call x1, Pallas kernels: 60.1 us -> 53.1 us  [shards(): pl.pallas_call(kernel, out_shape=jax.ShapeDtypeStruct((rows + 2, per_devi...]
where the time goes in v4:
time: 56.4 us; the launch traced here: 55.6 us
  Pallas kernels  55 us (98%)
  between operations  0.64 us (1%)
    pallas_call x1, Pallas kernels, shards(): pl.pallas_call(kernel, out_shape=jax.ShapeDtypeStruct((rows + 2, per_devi...  53.1 us
    pallas_call x1, Pallas kernels, shards(): pl.pallas_call(finish, grid=(per_device // part,), out_shape=[jax.ShapeDt...  1.88 us

profile of v4, /device:TPU:1, one launch (start us, length us, event | category | flops | bytes accessed | tf_op | source)
XLA Modules:
  0.0 55.6 jit_solution(11331120215995665983)
XLA Ops:
  0.6 53.1 %shard_map.59.field = bf16[34,16,128]{2,1,0:T(8,128)(2,1)} custom-call(bf16[3,16,128]{2,1,0:T(8,128)(2,1)} %bitcast.3, bf16[3,128,32,128]{3,2,1,0:T(8,128)(2,1)} %basis.1, s32[3,32]{1,0:T(4,128)} %bitcast.4, s32[1,32]{1,0:T(1,128)} %bitcast.5), custom_call_target="tpu_custom_call" | custom-call | tf_op jit(solution)/shard_map/pallas_call | solution.py:297
  53.7 1.9 %shard_map.60 = (f32[16,32,128]{2,1,0:T(8,128)}, f32[16,32,128]{2,1,0:T(8,128)}) custom-call(bf16[34,16,128]{2,1,0:T(8,128)(2,1)} %shard_map.59.field), custom_call_target="tpu_custom_call" | custom-call | tf_op jit(solution)/shard_map/pallas_call | solution.py:339

commit v5 on v4

--- a/solution.py
+++ b/solution.py
@@ -14,12 +14,11 @@
 PARTS = 2
 
 
-def swapped(tiles):
+def swapped(tiles, step=1, stop=2 * RING, blocks=2 * RING):
     lane = lax.broadcasted_iota(jnp.int32, tiles[0].shape, 1)
     count = len(tiles)
-    step = 1
-    while step < count:
-        width = step * (LANES // count)
+    while step < stop:
+        width = step * (LANES // blocks)
         low = (lane // width) % 2 == 0
         new = [None] * count
         for i in range(count):
@@ -35,7 +34,7 @@
 
 def kernel(
     coef, basis, shifts, owners, field,
-    rows_in, shift_in, owner_row, coefs, raw, modes, s1, r1, s2, r2, long, s3, r3, s4, r4,
+    rows_in, edges, shift_in, owner_row, coefs, raw, modes, s1, r1, s2, r2, e1, f1, e2, f2, long, s3, r3, s4, r4,
     p1, q1, p2, q2, p3, q3, p4, q4,
     basis_sem, small_sem, field_sem, send1, recv1, own1, send2, recv2, own2,
     send3, recv3, own3, send4, recv4, own4, halo_send, halo_recv,
@@ -76,21 +75,21 @@
         pl.semaphore_signal(barrier, inc=1, device_id=in_plane((seat + d) % plane), device_id_type=MESH)
         return carry
 
-    lax.fori_loop(0, RING - 1, greet_z, 0)
-    lax.fori_loop(1, plane, greet_plane, 0)
-    pl.semaphore_signal(barrier, inc=1, device_id={"loop": before}, device_id_type=MESH)
-    pl.semaphore_signal(barrier, inc=1, device_id={"loop": after}, device_id_type=MESH)
-
     frames = basis.shape[0]
+    loads = [pltpu.make_async_copy(basis.at[f], raw.at[f], basis_sem.at[f]) for f in range(frames)]
     small = [
         pltpu.make_async_copy(coef, coefs, small_sem.at[0]),
         pltpu.make_async_copy(owners, owner_row, small_sem.at[1]),
         pltpu.make_async_copy(shifts, shift_in, small_sem.at[2]),
     ]
-    loads = [pltpu.make_async_copy(basis.at[f], raw.at[f], basis_sem.at[f]) for f in range(frames)]
     loads[0].start()
-    for load in small + loads[1:]:
+    small[0].start()
+    lax.fori_loop(0, RING - 1, greet_z, 0, unroll=True)
+    for load in loads[1:] + small[1:]:
         load.start()
+    lax.fori_loop(1, plane, greet_plane, 0, unroll=True)
+    pl.semaphore_signal(barrier, inc=1, device_id={"loop": before}, device_id_type=MESH)
+    pl.semaphore_signal(barrier, inc=1, device_id={"loop": after}, device_id_type=MESH)
 
     def spread(source, target, here, to, send_sem, recv_sem, own_sem):
         pltpu.make_async_copy(source.at[here], target.at[here], own_sem).start()
@@ -103,7 +102,7 @@
             ).start()
             return carry
 
-        lax.fori_loop(0, RING - 1, one, 0)
+        lax.fori_loop(0, RING - 1, one, 0, unroll=True)
 
     def landed(source, target, here, recv_sem, own_sem):
         pltpu.make_async_copy(source.at[here], target.at[here], own_sem).wait()
@@ -128,7 +127,7 @@
             ).start()
             return carry
 
-        lax.fori_loop(1, plane, one, 0)
+        lax.fori_loop(1, plane, one, 0, unroll=True)
 
     def landed_plane(source, target, recv_sem, own_sem):
         pltpu.make_async_copy(source.at[spot], target.at[seat], own_sem).wait()
@@ -139,24 +138,27 @@
         most = target.at[pl.ds(0, plane - 1)]
         pltpu.make_async_copy(most, most, send_sem).wait()
 
-    last = frames
-    for f in range(frames):
-        loads[f].wait()
-        modes[f] = jnp.swapaxes(raw[f], 0, 1)
-        if f == 0:
-            small[0].wait()
-        weights = coefs[f]
-        tiles = [
-            jnp.dot(weights, modes[f, x], preferred_element_type=jnp.float32).astype(jnp.bfloat16)
-            for x in range(2 * RING)
-        ]
-        tiles = swapped(tiles)
-        for i in range(RING):
-            s1[f, i] = tiles[i]
-        if f == 0:
+    last = 2
+    early = frames - 1
+    trains = [(0, range(early), s1, r1, s2, r2), (1, range(early, frames), e1, f1, e2, f2)]
+    for k, members, out, into, _, _ in trains:
+        for f in members:
+            loads[f].wait()
+            modes[f] = jnp.swapaxes(raw[f], 0, 1)
+            if f == 0:
+                small[0].wait()
+            weights = coefs[f]
+            tiles = [
+                jnp.dot(weights, modes[f, x], preferred_element_type=jnp.float32).astype(jnp.bfloat16)
+                for x in range(2 * RING)
+            ]
+            tiles = swapped(tiles)
+            for i in range(RING):
+                out[i, f - members[0]] = tiles[i]
+            p1[:, f] = jnp.swapaxes(jnp.stack(tiles[RING:]), 0, 1)
+        if k == 0:
             pl.semaphore_wait(barrier, RING - 1 + plane - 1 + 2)
-        spread(s1.at[f], r1.at[f], z, at_z, send1.at[f], recv1.at[f], own1.at[f])
-        p1[:, f] = jnp.swapaxes(jnp.stack(tiles[RING:]), 0, 1)
+        spread(out, into, z, at_z, send1.at[k], recv1.at[k], own1.at[k])
     spread(p1, q1, spot, at_spot, send2.at[last], recv2.at[last], own2.at[last])
 
     queries = owners.shape[1]
@@ -210,14 +212,16 @@
         p2[:, f] = jnp.swapaxes(q1[:, f], 0, 1)
     spread(p2, q2, z, at_z, send1.at[last], recv1.at[last], own1.at[last])
 
-    for f in range(frames):
-        landed(s1.at[f], r1.at[f], z, recv1.at[f], own1.at[f])
-        s2[f] = jnp.swapaxes(r1[f], 0, 1)
-        spread(s2.at[f], r2.at[f], spot, at_spot, send2.at[f], recv2.at[f], own2.at[f])
-    for f in range(frames):
-        landed(s2.at[f], r2.at[f], spot, recv2.at[f], own2.at[f])
-        for i in range(RING):
-            store_long(0, f, i, r2[f, i])
+    for k, members, out, into, out2, _ in trains:
+        landed(out, into, z, recv1.at[k], own1.at[k])
+        for n in range(len(members)):
+            out2[:, n] = jnp.swapaxes(into[:, n], 0, 1)
+        spread(out2, trains[k][5], spot, at_spot, send2.at[k], recv2.at[k], own2.at[k])
+    for k, members, _, _, out2, into2 in trains:
+        landed(out2, into2, spot, recv2.at[k], own2.at[k])
+        for f in members:
+            for i in range(RING):
+                store_long(0, f, i, into2[i, f - members[0]])
     parts = summed(0)
     for i in range(RING):
         s3[i] = parts[i]
@@ -241,28 +245,42 @@
     p4[...] = jnp.swapaxes(q3[...], 0, 1)
     spread_plane(p4, q4, send3.at[1], recv3.at[1], own3.at[1])
 
+    length = 2 * RING
+    place = lax.broadcasted_iota(jnp.int32, (RING, LANES), 1) // WIDE
+
+    def edge(row, tiles, block, x):
+        for i, tile in enumerate(tiles):
+            row = jnp.where(place == block + i, pltpu.roll(tile, (block + i - x) * WIDE % LANES, 1), row)
+        return row
+
+    blank = jnp.zeros((RING, LANES), jnp.bfloat16)
     landed(s4, r4, z, recv4.at[0], own4.at[0])
+    early_tiles = [r4[i] for i in range(RING)]
+    first_row = edge(blank, early_tiles, 0, 0)
+    last_row = edge(blank, early_tiles, 0, length - 1)
+    early_tiles = swapped(early_tiles, 1, RING)
     landed_plane(p4, q4, recv3.at[1], own3.at[1])
-    tiles = swapped([r4[i] for i in range(RING)] + owned(q4[...]))
-    for x in range(2 * RING):
-        rows_in[x] = tiles[x]
-
-    length = 2 * RING
+    late_tiles = owned(q4[...])
+    edges[0] = edge(first_row, late_tiles, RING, 0)
+    edges[1] = edge(last_row, late_tiles, RING, length - 1)
     up = pltpu.make_async_remote_copy(
-        src_ref=rows_in.at[length - 1], dst_ref=field.at[0], send_sem=halo_send.at[0], recv_sem=halo_recv.at[0],
+        src_ref=edges.at[1], dst_ref=field.at[0], send_sem=halo_send.at[0], recv_sem=halo_recv.at[0],
         device_id={"loop": after}, device_id_type=MESH,
     )
     down = pltpu.make_async_remote_copy(
-        src_ref=rows_in.at[0], dst_ref=field.at[length + 1], send_sem=halo_send.at[1], recv_sem=halo_recv.at[1],
+        src_ref=edges.at[0], dst_ref=field.at[length + 1], send_sem=halo_send.at[1], recv_sem=halo_recv.at[1],
         device_id={"loop": before}, device_id_type=MESH,
     )
     up.start()
     down.start()
+    tiles = swapped(early_tiles + swapped(late_tiles, 1, RING), RING, length)
+    for x in range(length):
+        rows_in[x] = tiles[x]
     inside = pltpu.make_async_copy(rows_in, field.at[pl.ds(1, length)], field_sem)
     inside.start()
-    for f in range(frames):
-        sent(s1.at[f], send1.at[f])
-        sent(s2.at[f], send2.at[f])
+    for k, _, out, _, out2, _ in trains:
+        sent(out, send1.at[k])
+        sent(out2, send2.at[k])
     sent(p1, send2.at[last])
     sent(p2, send1.at[last])
     sent_plane(r3, send3.at[0])
@@ -301,15 +319,20 @@
         out_specs=hbm,
         scratch_shapes=[
             pltpu.VMEM((rows, per_device, cells), bf16),
+            pltpu.VMEM((2, per_device, cells), bf16),
             pltpu.SMEM((frames, queries), jnp.int32),
             pltpu.VMEM((1, queries), jnp.int32),
             pltpu.VMEM((frames, per_device, modes), bf16),
             pltpu.VMEM((frames, modes, rows, cells), bf16),
             pltpu.VMEM((frames, rows, modes, cells), bf16),
-            pltpu.VMEM((frames,) + block, bf16),
-            pltpu.VMEM((frames,) + block, bf16),
-            pltpu.VMEM((frames,) + block, bf16),
-            pltpu.VMEM((frames,) + block, bf16),
+            pltpu.VMEM((RING, frames - 1, RING, LANES), bf16),
+            pltpu.VMEM((RING, frames - 1, RING, LANES), bf16),
+            pltpu.VMEM((RING, frames - 1, RING, LANES), bf16),
+            pltpu.VMEM((RING, frames - 1, RING, LANES), bf16),
+            pltpu.VMEM((RING, 1, RING, LANES), bf16),
+            pltpu.VMEM((RING, 1, RING, LANES), bf16),
+            pltpu.VMEM((RING, 1, RING, LANES), bf16),
+            pltpu.VMEM((RING, 1, RING, LANES), bf16),
             pltpu.VMEM((PARTS, frames, 2, 256, LANES), f32),
             pltpu.VMEM(block, bf16),
             pltpu.VMEM((2 * RING, RING, LANES), bf16),
@@ -324,8 +347,8 @@
             pltpu.VMEM(block, bf16),
             pltpu.VMEM((2 * RING, RING, LANES), bf16),
             dma((frames,)), dma((3,)), dma(()),
-            dma((frames + 1,)), dma((frames + 1,)), dma((frames + 1,)),
-            dma((frames + 1,)), dma((frames + 1,)), dma((frames + 1,)),
+            dma((3,)), dma((3,)), dma((3,)),
+            dma((3,)), dma((3,)), dma((3,)),
             dma((PARTS,)), dma((PARTS,)), dma((PARTS,)),
             dma((PARTS,)), dma((PARTS,)), dma((PARTS,)),
             dma((2,)), dma((2,)),

time: 56.4 us -> 56 us (level); the launches traced: 55.6 us -> 55.8 us
  no operation moved by 1% of the time
where the time goes in v5:
time: 56 us; the launch traced here: 55.8 us
  Pallas kernels  55.2 us (99%)
  between operations  0.64 us (1%)
    pallas_call x1, Pallas kernels, shards(): pl.pallas_call(kernel, out_shape=jax.ShapeDtypeStruct((rows + 2, per_devi...  53.3 us
    pallas_call x1, Pallas kernels, shards(): pl.pallas_call(finish, grid=(per_device // part,), out_shape=[jax.ShapeDt...  1.88 us

profile of v5, /device:TPU:1, one launch (start us, length us, event | category | flops | bytes accessed | tf_op | source)
XLA Modules:
  0.0 55.8 jit_solution(14084553295188234191)
XLA Ops:
  0.6 53.3 %shard_map.59.field = bf16[34,16,128]{2,1,0:T(8,128)(2,1)} custom-call(bf16[3,16,128]{2,1,0:T(8,128)(2,1)} %bitcast.3, bf16[3,128,32,128]{3,2,1,0:T(8,128)(2,1)} %basis.1, s32[3,32]{1,0:T(4,128)} %bitcast.4, s32[1,32]{1,0:T(1,128)} %bitcast.5), custom_call_target="tpu_custom_call" | custom-call | tf_op jit(solution)/shard_map/pallas_call | solution.py:315
  53.9 1.9 %shard_map.60 = (f32[16,32,128]{2,1,0:T(8,128)}, f32[16,32,128]{2,1,0:T(8,128)}) custom-call(bf16[34,16,128]{2,1,0:T(8,128)(2,1)} %shard_map.59.field), custom_call_target="tpu_custom_call" | custom-call | tf_op jit(solution)/shard_map/pallas_call | solution.py:362

commit v6 on v5

--- a/solution.py
+++ b/solution.py
@@ -158,8 +158,9 @@
             p1[:, f] = jnp.swapaxes(jnp.stack(tiles[RING:]), 0, 1)
         if k == 0:
             pl.semaphore_wait(barrier, RING - 1 + plane - 1 + 2)
+        else:
+            spread(p1, q1, spot, at_spot, send2.at[last], recv2.at[last], own2.at[last])
         spread(out, into, z, at_z, send1.at[k], recv1.at[k], own1.at[k])
-    spread(p1, q1, spot, at_spot, send2.at[last], recv2.at[last], own2.at[last])
 
     queries = owners.shape[1]
     small[1].wait()

time: 56 us -> 56.2 us (level)
  no operation moved by 1% of the time
where the time goes in v6:
time: 56.2 us; the launch traced here: 56 us
  Pallas kernels  55.4 us (99%)
  between operations  0.64 us (1%)
    pallas_call x1, Pallas kernels, shards(): pl.pallas_call(kernel, out_shape=jax.ShapeDtypeStruct((rows + 2, per_devi...  53.5 us
    pallas_call x1, Pallas kernels, shards(): pl.pallas_call(finish, grid=(per_device // part,), out_shape=[jax.ShapeDt...  1.88 us

profile of v6, /device:TPU:1, one launch (start us, length us, event | category | flops | bytes accessed | tf_op | source)
XLA Modules:
  0.0 56.0 jit_solution(2109908235106670220)
XLA Ops:
  0.6 53.5 %shard_map.59.field = bf16[34,16,128]{2,1,0:T(8,128)(2,1)} custom-call(bf16[3,16,128]{2,1,0:T(8,128)(2,1)} %bitcast.3, bf16[3,128,32,128]{3,2,1,0:T(8,128)(2,1)} %basis.1, s32[3,32]{1,0:T(4,128)} %bitcast.4, s32[1,32]{1,0:T(1,128)} %bitcast.5), custom_call_target="tpu_custom_call" | custom-call | tf_op jit(solution)/shard_map/pallas_call | solution.py:316
  54.2 1.9 %shard_map.60 = (f32[16,32,128]{2,1,0:T(8,128)}, f32[16,32,128]{2,1,0:T(8,128)}) custom-call(bf16[34,16,128]{2,1,0:T(8,128)(2,1)} %shard_map.59.field), custom_call_target="tpu_custom_call" | custom-call | tf_op jit(solution)/shard_map/pallas_call | solution.py:363

commit v7 on v5

--- a/solution.py
+++ b/solution.py
@@ -76,16 +76,21 @@
         return carry
 
     frames = basis.shape[0]
-    loads = [pltpu.make_async_copy(basis.at[f], raw.at[f], basis_sem.at[f]) for f in range(frames)]
+    depth = basis.shape[1] // 2
+    loads = [
+        pltpu.make_async_copy(basis.at[f, pl.ds(p * depth, depth)], raw.at[f, pl.ds(p * depth, depth)], basis_sem.at[f, p])
+        for f in range(frames) for p in range(2)
+    ]
     small = [
         pltpu.make_async_copy(coef, coefs, small_sem.at[0]),
         pltpu.make_async_copy(owners, owner_row, small_sem.at[1]),
         pltpu.make_async_copy(shifts, shift_in, small_sem.at[2]),
     ]
     loads[0].start()
+    loads[1].start()
     small[0].start()
     lax.fori_loop(0, RING - 1, greet_z, 0, unroll=True)
-    for load in loads[1:] + small[1:]:
+    for load in loads[2:] + small[1:]:
         load.start()
     lax.fori_loop(1, plane, greet_plane, 0, unroll=True)
     pl.semaphore_signal(barrier, inc=1, device_id={"loop": before}, device_id_type=MESH)
@@ -143,7 +148,8 @@
     trains = [(0, range(early), s1, r1, s2, r2), (1, range(early, frames), e1, f1, e2, f2)]
     for k, members, out, into, _, _ in trains:
         for f in members:
-            loads[f].wait()
+            loads[2 * f].wait()
+            loads[2 * f + 1].wait()
             modes[f] = jnp.swapaxes(raw[f], 0, 1)
             if f == 0:
                 small[0].wait()
@@ -346,7 +352,7 @@
             pltpu.VMEM(block, bf16),
             pltpu.VMEM(block, bf16),
             pltpu.VMEM((2 * RING, RING, LANES), bf16),
-            dma((frames,)), dma((3,)), dma(()),
+            dma((frames, 2)), dma((3,)), dma(()),
             dma((3,)), dma((3,)), dma((3,)),
             dma((3,)), dma((3,)), dma((3,)),
             dma((PARTS,)), dma((PARTS,)), dma((PARTS,)),

time: 56 us -> 56.3 us (level)
  no operation moved by 1% of the time
where the time goes in v7:
time: 56.3 us; the launch traced here: 56.1 us
  Pallas kernels  55.5 us (99%)
  between operations  0.64 us (1%)
    pallas_call x1, Pallas kernels, shards(): pl.pallas_call(kernel, out_shape=jax.ShapeDtypeStruct((rows + 2, per_devi...  53.6 us
    pallas_call x1, Pallas kernels, shards(): pl.pallas_call(finish, grid=(per_device // part,), out_shape=[jax.ShapeDt...  1.88 us

profile of v7, /device:TPU:1, one launch (start us, length us, event | category | flops | bytes accessed | tf_op | source)
XLA Modules:
  0.0 56.1 jit_solution(12543404061290924803)
XLA Ops:
  0.6 53.6 %shard_map.59.field = bf16[34,16,128]{2,1,0:T(8,128)(2,1)} custom-call(bf16[3,16,128]{2,1,0:T(8,128)(2,1)} %bitcast.3, bf16[3,128,32,128]{3,2,1,0:T(8,128)(2,1)} %basis.1, s32[3,32]{1,0:T(4,128)} %bitcast.4, s32[1,32]{1,0:T(1,128)} %bitcast.5), custom_call_target="tpu_custom_call" | custom-call | tf_op jit(solution)/shard_map/pallas_call | solution.py:321
  54.2 1.9 %shard_map.60 = (f32[16,32,128]{2,1,0:T(8,128)}, f32[16,32,128]{2,1,0:T(8,128)}) custom-call(bf16[34,16,128]{2,1,0:T(8,128)(2,1)} %shard_map.59.field), custom_call_target="tpu_custom_call" | custom-call | tf_op jit(solution)/shard_map/pallas_call | solution.py:368
